TPU v7x, 32 devices: a whole 2x2x4 slice. The times are simulated.
32 devices in a mesh: videos: 2 (over x), rows: 16 (over z, y, core).
Axes of the slice: x: 2, y: 2, z: 4, core: 2. Of those that a mesh axis runs over, the one named last changes fastest.
Arguments:
- latents: bfloat16 [4, 32, 64, 384], P('videos', 'rows'), parts along dimension 0, may hold values from -6 to 6
- conv_cache: bfloat16 [4, 32, 64, 384], P('videos', 'rows'), parts along dimension 0, may hold values from -4 to 4
- norm_gain: float32 [384], replicated, may hold values from 0.1 to 1.9
- conv_weight: bfloat16 [3, 3, 3, 384, 384], replicated, may hold values from -0.0625 to 0.0625
- attn_gain: float32 [384], replicated, may hold values from 0.1 to 1.9
- query_weight: bfloat16 [384, 384], replicated, may hold values from -3 to 3
- key_weight: bfloat16 [384, 384], replicated, may hold values from -3 to 3
- value_weight: bfloat16 [384, 384], replicated, may hold values from -0.3125 to 0.3125
- out_weight: bfloat16 [384, 384], replicated, may hold values from -0.3125 to 0.3125
- up_weight: bfloat16 [3, 3, 384, 192], replicated, may hold values from -0.109375 to 0.109375
Outputs:
- decoded: bfloat16 [4, 64, 128, 192], P('videos', 'rows'), parts along dimension 0
- next_cache: bfloat16 [4, 32, 64, 384], P('videos', 'rows'), parts along dimension 0
There are 2 independent parts, one for each index of `videos`. A program takes and returns all parts, laid end to end along the dimension named above; an argument that names none is the same for every part. Nothing has to cross between parts.
All inputs are finite; a program needn't handle non-finite values.
Results may differ from a plain program's by a relative error of at most 0.0058.
Values may be sent and summed in bfloat16 or wider, within the bound.
No kernel may reach another device: no remote copies, remote signals or barrier semaphores. Data moves between devices by JAX's collectives and lax.ppermute only.
A program may use at most 128 MiB of HBM per device.

v0:
```python
import functools

import jax
import jax.numpy as jnp
from jax import lax
from jax.experimental import pallas as pl
from jax.experimental.pallas import tpu as pltpu
from jax.sharding import PartitionSpec as P

BF16 = jnp.bfloat16
F32 = jnp.float32
EPS = 1e-06
MIB = 1024 * 1024
EXTRA = 16


def normalize(values, gain):
    return values * lax.rsqrt(jnp.mean(values * values, axis=-1, keepdims=True) + EPS) * gain


def activate(values, gain):
    normed = normalize(values.astype(F32), gain)
    return (normed / (1.0 + jnp.exp(-normed))).astype(BF16)


def vmem():
    return pl.BlockSpec(memory_space=pltpu.VMEM)


def params(mib):
    return pltpu.CompilerParams(vmem_limit_bytes=mib * MIB)


def cost(flops, size, exps=0):
    return pl.CostEstimate(flops=flops, bytes_accessed=size, transcendentals=exps)


def edges_kernel(latents_ref, cache_ref, edge_ref, both_ref, sems):
    core = lax.axis_index("rows") % 2
    row = core * (latents_ref.shape[1] - 1)
    copies = [
        pltpu.make_async_copy(cache_ref.at[:, row], edge_ref.at[pl.ds(0, 2)], sems.at[0]),
        pltpu.make_async_copy(latents_ref.at[:, row], edge_ref.at[pl.ds(2, 2)], sems.at[1]),
        pltpu.make_async_copy(cache_ref.at[1], both_ref.at[core], sems.at[2]),
        pltpu.make_async_copy(latents_ref.at[0], both_ref.at[1 + core], sems.at[3]),
    ]
    for copy in copies:
        copy.start()

    @pl.when(core == 0)
    def _():
        last = pltpu.make_async_copy(latents_ref.at[1], both_ref.at[2], sems.at[4])
        last.start()
        last.wait()

    @pl.when(core == 1)
    def _():
        last = pltpu.make_async_copy(cache_ref.at[0], both_ref.at[0], sems.at[4])
        last.start()
        last.wait()

    for copy in copies:
        copy.wait()


def start_all(pairs, sems, first=0):
    copies = [
        pltpu.make_async_copy(source, target, sems.at[first + i])
        for i, (source, target) in enumerate(pairs)
    ]
    for copy in copies:
        copy.start()
    return copies


def wait_all(copies):
    for copy in copies:
        copy.wait()


def prepare_kernel(
    latents_ref,
    cache_ref,
    weight_ref,
    gain_ref,
    act_ref,
    own_ref,
    staged_ref,
    latents,
    cache,
    gain,
    act,
    sems,
):
    channels = latents_ref.shape[-1]
    core = lax.axis_index("rows") % 2
    loads = start_all([(latents_ref, latents), (cache_ref, cache), (gain_ref, gain)], sems)
    stages = start_all(
        [
            (
                weight_ref.at[time, :, col],
                staged_ref.at[time, :, :, pl.ds(col * channels, channels)],
            )
            for time in range(3)
            for col in range(3)
        ],
        sems,
        4,
    )
    wait_all(loads)
    act[...] = activate(latents[...], gain[...].reshape(1, channels))
    store = start_all([(act, act_ref)], sems, 3)
    own_ref[0] = cache[core]
    own_ref[1] = jnp.where(core == 0, cache[1], latents[0])
    own_ref[2] = latents[core]
    wait_all(store + stages)


def conv_kernel(
    width,
    own_ref,
    swap_ref,
    edge_ref,
    far_ref,
    norm_gain_ref,
    attn_gain_ref,
    weights,
    sent_ref,
    front_ref,
    back_ref,
    resid_ref,
    raw,
    second,
    third,
    total,
):
    channels = own_ref.shape[-1]
    core = lax.axis_index("rows") % 2
    own = 2 * width
    span = 4 * width
    gain = norm_gain_ref[...].reshape(1, channels)

    def put(index, values):
        rows = pl.ds(pl.multiple_of(index * width, width), values.shape[1])
        raw[:, rows, :] = values

    put(1 + 2 * core, own_ref[...])
    put(3 - 2 * core, swap_ref[...])
    put(5 * core, edge_ref[pl.ds(core, 3)])
    put(5 * (1 - core), far_ref[pl.ds(core, 3)])

    def taps(ref, time):
        lhs = jnp.concatenate([ref[row * width : row * width + span] for row in range(3)], axis=1)
        rhs = weights[time].reshape(3 * channels, 3 * channels)
        return jnp.dot(lhs, rhs, preferred_element_type=F32)

    total[...] = taps(raw.at[0], 0)
    second[...] = jnp.where(core == 1, activate(raw[1], gain), raw[1])
    third[...] = activate(raw[2], gain)
    total[...] += taps(second, 1)
    total[...] += taps(third, 2)

    column = lax.broadcasted_iota(jnp.int32, (span, 1), 0) % width
    left = pltpu.roll(total[:, :channels], 1, axis=0)
    right = pltpu.roll(total[:, 2 * channels :], span - 1, axis=0)
    conv_out = total[:, channels : 2 * channels]
    conv_out = conv_out + jnp.where(column == 0, 0.0, left)
    conv_out = conv_out + jnp.where(column == width - 1, 0.0, right)
    resid = raw[2, width : width + span].astype(F32) + conv_out
    resid_ref[...] = resid
    size = jnp.mean(resid * resid, axis=-1, keepdims=True) + EPS
    normed = resid * lax.rsqrt(size) * attn_gain_ref[...].reshape(1, channels)
    edges = jnp.sqrt(jnp.concatenate([size[:width], size[span - width :]], axis=0))
    across = jnp.transpose(jnp.broadcast_to(edges, (2 * width, 128)))[:EXTRA]
    high = across.astype(BF16).astype(F32)
    line = lax.broadcasted_iota(jnp.int32, (EXTRA, 1), 0)
    extra = jnp.where(line == 0, high, jnp.where(line == 1, across - high, 0.0)).astype(BF16)
    half = span // 2
    for ref, low, count in ((sent_ref, 0, span), (front_ref, 0, half), (back_ref, half, half)):
        ref[:count] = normed[low : low + count].astype(BF16)
        ref[count:] = jnp.zeros((EXTRA, channels), BF16)
        ref[count:, : 2 * width] = extra


def nt_dot(a, b):
    return lax.dot_general(a, b, (((1,), (1,)), ((), ())), preferred_element_type=F32)


def whole(parts):
    rows = [part[: part.shape[0] - EXTRA] for part in parts]
    return rows[0] if len(rows) == 1 else jnp.concatenate(rows, axis=0)


def grouped(refs, counts):
    blocks, first = [], 0
    for count in counts:
        blocks.append(refs[first : first + count])
        first += count
    return blocks


def fold(values, combine, total):
    for lane in range(0, values.shape[1], 128):
        piece = values[:, lane : lane + 128]
        total = piece if total is None else combine(total, piece)
    return total


def attend(queries, keys, scores, start, peak, sums, added):
    height = queries.shape[0]
    top = None
    for i, key in enumerate(keys):
        part = nt_dot(queries, key)
        scores[i, start : start + height] = part
        top = fold(part, jnp.maximum, top)
    top = jnp.max(top, axis=-1, keepdims=True)
    if peak is not None:
        top = jnp.maximum(top, peak)
        shrink = jnp.exp2(peak - top)
        sums = sums * shrink
        added = added * shrink
    for i, key in enumerate(keys):
        weights = jnp.exp2(scores[i, start : start + height] - top)
        sums = fold(weights, jnp.add, sums)
        part = jnp.dot(weights.astype(BF16), key, preferred_element_type=F32)
        added = part if added is None else added + part
    return top, sums, added


def fuse_kernel(scale, query_ref, key_ref, value_ref, out_ref, score_ref, mix_ref):
    score_ref[...] = (nt_dot(query_ref[...], key_ref[...]) * scale).astype(BF16)
    mix_ref[...] = jnp.dot(
        value_ref[...], out_ref[...], preferred_element_type=F32
    ).astype(BF16)


def lead(rows, score_weight):
    return jnp.dot(rows, score_weight[...], preferred_element_type=F32).astype(BF16)


def early_kernel(counts, score_ref, *refs):
    blocks = grouped(refs, counts)
    own_query_ref, peak_ref, sums_ref, added_ref, scores = refs[-5:]
    keys = [whole(parts) for parts in blocks]
    queries = lead(keys[0], score_ref)
    own_query_ref[...] = queries
    peak, sums, added = attend(queries, keys, scores, 0, None, None, None)
    peak_ref[...] = jnp.broadcast_to(peak, peak_ref.shape)
    sums_ref[...] = sums
    added_ref[...] = added


def late_kernel(
    width,
    sources,
    counts,
    early,
    own_query_ref,
    peak_ref,
    sums_ref,
    added_ref,
    resid_ref,
    gain_ref,
    score_ref,
    mix_weight_ref,
    *refs,
):
    blocks = grouped(refs, counts)
    mid_ref, swap_ref, scores, mid, halo, sizes = refs[sum(counts) :]
    place = lax.axis_index("rows")
    core = place % 2
    chip = place // 2
    own, channels = own_query_ref.shape
    chips = len(sources[0])

    for block, origin in zip(blocks, sources):
        for step, part, low in ((-1, block[-1], 0), (1, block[0], width)):
            rows = part.shape[0] - EXTRA
            first = rows - width if step < 0 else 0
            takers = [k for k in range(chips) if origin[k] == k + step]
            if not takers:
                continue
            wanted = chip == takers[0]
            for k in takers[1:]:
                wanted = jnp.logical_or(wanted, chip == k)

            @pl.when(wanted)
            def _(part=part, rows=rows, first=first, low=low):
                halo[low : low + width] = part[first : first + width, :]
                sizes[low // width] = part[rows : rows + EXTRA, : 2 * width]

    no_above = chip == 0
    no_below = chip == chips - 1

    @pl.when(no_above)
    def _():
        halo[:width] = jnp.zeros((width, channels), BF16)
        sizes[0] = jnp.zeros((EXTRA, 2 * width), BF16)

    @pl.when(no_below)
    def _():
        halo[width:] = jnp.zeros((width, channels), BF16)
        sizes[1] = jnp.zeros((EXTRA, 2 * width), BF16)

    def column(index):
        parts = sizes[index].astype(F32)
        line = parts[0:1] + parts[1:2]
        return jnp.transpose(jnp.broadcast_to(line, (128, 2 * width)))[:, :1]

    edge_rows = halo[...]
    edge_size = jnp.concatenate([column(0)[width:], column(1)[:width]], axis=0)
    edge_resid = edge_rows.astype(F32) * edge_size / gain_ref[...].reshape(1, channels)
    edge_query = lead(edge_rows, score_ref)
    keys = [whole(parts) for parts in blocks]
    _, edge_sums, edge_added = attend(edge_query, keys, scores, own, None, None, None)
    _, own_sums, own_added = attend(
        own_query_ref[...],
        keys[early:],
        scores,
        0,
        peak_ref[:, :1],
        sums_ref[...],
        added_ref[...],
    )

    def finish(added, sums):
        return (added / jnp.sum(sums, axis=-1, keepdims=True)).astype(BF16)

    mixed = jnp.concatenate([finish(own_added, own_sums), finish(edge_added, edge_sums)], axis=0)
    projected = jnp.dot(mixed, mix_weight_ref[...], preferred_element_type=F32)
    inner = own + width
    mid[width:inner] = (resid_ref[...] + projected[:own]).astype(BF16)
    edges = edge_resid + projected[own:]
    mid[:width] = jnp.where(no_above, 0.0, edges[:width]).astype(BF16)
    mid[inner:] = jnp.where(no_below, 0.0, edges[width:]).astype(BF16)
    mid_ref[...] = mid[pl.ds(pl.multiple_of(2 * core * width, width), 4 * width), :]
    swap_ref[...] = mid[pl.ds(pl.multiple_of(2 * (1 - core) * width, width), 4 * width), :]


def up_kernel(width, mid_ref, swap_ref, weight_ref, out_ref, fine, total, results, sems):
    core = lax.axis_index("rows") % 2
    channels = mid_ref.shape[1]
    outputs = weight_ref.shape[2]
    wide = 2 * width
    lane = lax.broadcasted_iota(jnp.int32, (1, wide), 1)
    lhs = weight_ref[...].reshape(9 * outputs, channels)
    stores = []
    for slot, ref, frame in ((0, mid_ref, core), (1, swap_ref, 1 - core)):
        values = ref[...].astype(F32)
        pieces = []
        for i in range(channels // 128):
            piece = values[:, 128 * i : 128 * (i + 1)]
            fine[slot, i, pl.ds(0, 4 * width, stride=2), :] = piece
            fine[slot, i, pl.ds(1, 4 * width, stride=2), :] = piece
            pieces.append(fine[slot, i].astype(BF16))
        total[slot] = nt_dot(lhs, jnp.concatenate(pieces, axis=1))
        for row in range(4):
            low = row // 2 + 1
            picks = (low - 1, low, low) if row % 2 == 0 else (low, low, low + 1)
            taps = []
            for col in range(3):
                tap = None
                for j, pick in enumerate(picks):
                    piece = total[
                        slot,
                        (3 * j + col) * outputs : (3 * j + col + 1) * outputs,
                        pick * wide : (pick + 1) * wide,
                    ]
                    tap = piece if tap is None else tap + piece
                taps.append(tap)
            result = taps[1]
            result = result + jnp.where(lane == 0, 0.0, pltpu.roll(taps[0], 1, axis=1))
            result = result + jnp.where(
                lane == wide - 1, 0.0, pltpu.roll(taps[2], wide - 1, axis=1)
            )
            results[slot, row] = result.astype(BF16)
        stores = stores + start_all([(results.at[slot], out_ref.at[frame])], sems, slot)
    wait_all(stores)


def gather_blocks(block, halves, count):
    chips = count // 2
    depth = 2 if chips % 2 == 0 else 1
    length = chips // depth

    ring = [0] + list(range(1, length, 2)) + list(range(2, length, 2))[::-1]
    follow = {a: ring[(i + 1) % length] for i, a in enumerate(ring)}
    onward = {a * depth + b: follow[a] * depth + b for a in range(length) for b in range(depth)}
    backward = {target: source for source, target in onward.items()}
    across = {k: k ^ 1 for k in range(chips)}

    def send(parts, targets):
        pairs = [(2 * k + c, 2 * targets[k] + c) for k in range(chips) for c in range(2)]
        return [lax.ppermute(part, "rows", pairs) for part in parts]

    def moved(origin, targets):
        return {targets[k]: origin[k] for k in range(chips)}

    def tie(*places):
        fixed = lax.optimization_barrier(tuple(where[i] for where, i in places))
        for (where, i), value in zip(places, fixed):
            where[i] = value

    here = {k: k for k in range(chips)}
    early, late = [([block], here)], []
    own_again = [block]
    crossed = last = None
    if depth == 2:
        crossed = send([block], across)
    steps = length - 2
    parts, origin = list(halves), here
    for step in range(1, steps + 1):
        parts, origin = send(parts, onward), moved(origin, onward)
        for h in range(2):
            places = [(parts, h)]
            if last:
                places.append((last, h))
            if step == 1 and h == 1:
                places.append((own_again, 0))
                if depth == 2:
                    places.append((crossed, 0))
            tie(*places)
        early.append((parts, origin))
        if depth == 2:
            last = send(parts, across)
            (late if step == steps else early).append((last, moved(origin, across)))
    if length > 1:
        late.append((send(own_again, backward), moved(here, backward)))
    if depth == 2:
        (early if length > 1 else late).append((crossed, moved(here, across)))
        if length > 1:
            if steps > 0:
                crossed = list(crossed)
                tie((crossed, 0), (parts, 0))
            late.append((send(crossed, backward), moved(moved(here, across), backward)))
    return early, late


def shards(
    latents,
    conv_cache,
    norm_gain,
    conv_weight,
    attn_gain,
    query_weight,
    key_weight,
    value_weight,
    out_weight,
    up_weight,
):
    frames, rows_here, width, channels = latents.shape
    outputs = up_weight.shape[3]
    count = lax.axis_size("rows")
    span = 2 * rows_here * width
    own = rows_here * width
    edge = jax.ShapeDtypeStruct((width, channels), BF16)
    anywhere = pl.BlockSpec(memory_space=pl.ANY)
    hbm = pl.BlockSpec(memory_space=pltpu.HBM)

    chips = count // 2
    swap = [(2 * k + c, 2 * k + 1 - c) for k in range(chips) for c in range(2)]
    neighbour = [(2 * k + 1, 2 * k + 2) for k in range(chips - 1)]
    neighbour = neighbour + [(target, source) for source, target in neighbour]

    latents_in = pltpu.with_memory_space_constraint(latents, pltpu.HBM)
    cache_in = pltpu.with_memory_space_constraint(conv_cache, pltpu.HBM)
    edge_rows, both = pl.pallas_call(
        edges_kernel,
        out_shape=(
            jax.ShapeDtypeStruct((2 * frames, width, channels), BF16),
            jax.ShapeDtypeStruct((3, rows_here, width, channels), BF16),
        ),
        in_specs=[hbm] * 2,
        out_specs=(anywhere,) * 2,
        scratch_shapes=[pltpu.SemaphoreType.DMA((5,))],
        cost_estimate=cost(0, 20 * width * channels),
        compiler_params=params(4),
    )(latents_in, cache_in)
    edge_rows = lax.ppermute(edge_rows, "rows", neighbour)
    both = lax.ppermute(both, "rows", swap)
    act, own_rows, staged = pl.pallas_call(
        prepare_kernel,
        out_shape=(
            jax.ShapeDtypeStruct((frames, own, channels), BF16),
            jax.ShapeDtypeStruct((3, own, channels), BF16),
            jax.ShapeDtypeStruct((3, 3, channels, 3 * channels), BF16),
        ),
        in_specs=[hbm] * 4,
        out_specs=(anywhere, vmem(), anywhere),
        scratch_shapes=[
            pltpu.VMEM((frames, own, channels), BF16),
            pltpu.VMEM((frames, own, channels), BF16),
            pltpu.VMEM((channels,), F32),
            pltpu.VMEM((frames, own, channels), BF16),
            pltpu.SemaphoreType.DMA((13,)),
        ],
        cost_estimate=cost(10 * frames * own * channels, 2 * 27 * channels * channels),
        compiler_params=params(8),
    )(
        pltpu.with_memory_space_constraint(latents.reshape(frames, own, channels), pltpu.HBM),
        pltpu.with_memory_space_constraint(conv_cache.reshape(frames, own, channels), pltpu.HBM),
        pltpu.with_memory_space_constraint(conv_weight, pltpu.HBM),
        pltpu.with_memory_space_constraint(norm_gain, pltpu.HBM),
    )

    edge_rows, own_rows = lax.optimization_barrier((edge_rows, own_rows))
    far_rows = lax.ppermute(edge_rows, "rows", swap)
    block = jax.ShapeDtypeStruct((span + EXTRA, channels), BF16)
    half = jax.ShapeDtypeStruct((span // 2 + EXTRA, channels), BF16)
    sent, front, back, resid = pl.pallas_call(
        functools.partial(conv_kernel, width),
        out_shape=(block, half, half, jax.ShapeDtypeStruct((span, channels), F32)),
        in_specs=[vmem()] * 7,
        out_specs=(vmem(),) * 4,
        scratch_shapes=[
            pltpu.VMEM((3, 6 * width, channels), BF16),
            pltpu.VMEM((6 * width, channels), BF16),
            pltpu.VMEM((6 * width, channels), BF16),
            pltpu.VMEM((span, 3 * channels), F32),
        ],
        cost_estimate=cost(2 * 27 * span * channels * channels, 2 * 27 * channels * channels),
        compiler_params=params(20),
    )(
        own_rows,
        both.reshape(3, own, channels),
        edge_rows,
        far_rows,
        norm_gain,
        attn_gain,
        staged,
    )

    early, late = gather_blocks(sent, (front, back), count)
    blocks = early + late
    sources = [[origin[k] for k in range(chips)] for _, origin in blocks]
    counts = [len(parts) for parts, _ in blocks]
    early_parts = [part for parts, _ in early for part in parts]
    all_parts = [part for parts, _ in blocks for part in parts]

    scale = channels ** (-0.5) * 1.4426950408889634
    square = jax.ShapeDtypeStruct((channels, channels), BF16)
    score_weight, mix_weight = pl.pallas_call(
        functools.partial(fuse_kernel, scale),
        out_shape=(square, square),
        in_specs=[vmem()] * 4,
        out_specs=(vmem(),) * 2,
        cost_estimate=cost(4 * channels**3, 12 * channels * channels),
        compiler_params=params(8),
    )(query_weight, key_weight, value_weight, out_weight)

    wide = span + 2 * width
    lanes = jax.ShapeDtypeStruct((span, 128), F32)
    own_query, peak, sums, added = pl.pallas_call(
        functools.partial(early_kernel, counts[: len(early)]),
        out_shape=(
            jax.ShapeDtypeStruct((span, channels), BF16),
            lanes,
            lanes,
            jax.ShapeDtypeStruct((span, channels), F32),
        ),
        in_specs=[vmem()] * (1 + len(early_parts)),
        out_specs=(vmem(),) * 4,
        scratch_shapes=[pltpu.VMEM((len(early), span, span), F32)],
        cost_estimate=cost(
            4 * span * span * len(early) * channels,
            2 * span * channels * len(early),
            span * span * len(early),
        ),
        compiler_params=params(24),
    )(score_weight, *early_parts)

    mid, swap_rows = pl.pallas_call(
        functools.partial(late_kernel, width, sources, counts, len(early)),
        out_shape=(jax.ShapeDtypeStruct((4 * width, channels), BF16),) * 2,
        in_specs=[vmem()] * (8 + len(all_parts)),
        out_specs=(vmem(),) * 2,
        scratch_shapes=[
            pltpu.VMEM((len(blocks), wide, span), F32),
            pltpu.VMEM((wide, channels), BF16),
            pltpu.VMEM((2 * width, channels), BF16),
            pltpu.VMEM((2, EXTRA, 2 * width), BF16),
        ],
        cost_estimate=cost(
            2 * wide * span * len(blocks) * channels,
            2 * span * channels * len(blocks),
            wide * span * len(blocks) // 2,
        ),
        compiler_params=params(28),
    )(
        own_query,
        peak,
        sums,
        added,
        resid,
        attn_gain,
        score_weight,
        mix_weight,
        *all_parts,
    )

    swap_rows = lax.ppermute(swap_rows, "rows", swap)

    fine_shape = (2 * rows_here, outputs, 2 * width)
    decoded = pl.pallas_call(
        functools.partial(up_kernel, width),
        out_shape=jax.ShapeDtypeStruct((frames, *fine_shape), BF16),
        in_specs=[vmem()] * 3,
        out_specs=anywhere,
        scratch_shapes=[
            pltpu.VMEM((2, channels // 128, 8 * width, 128), F32),
            pltpu.VMEM((2, 9 * outputs, 8 * width), F32),
            pltpu.VMEM((2, *fine_shape), BF16),
            pltpu.SemaphoreType.DMA((2,)),
        ],
        cost_estimate=cost(
            2 * 9 * outputs * channels * 16 * width, 2 * 9 * outputs * channels
        ),
        compiler_params=params(24),
    )(mid, swap_rows, jnp.transpose(up_weight, (0, 1, 3, 2)))
    decoded = jnp.transpose(decoded, (0, 1, 3, 2))
    return (decoded, act.reshape(frames, rows_here, width, channels))


def solution(mesh):
    return jax.shard_map(
        shards,
        mesh=mesh,
        in_specs=(
            P("videos", "rows", None, None),
            P("videos", "rows", None, None),
            P(),
            P(),
            P(),
            P(),
            P(),
            P(),
            P(),
            P(),
        ),
        out_specs=(P("videos", "rows", None, None), P("videos", "rows", None, None)),
        check_vma=False,
    )
```

profile of v0, /device:TPU:25, one launch (start us, length us, event | category | flops | bytes accessed | tf_op | source)
XLA Modules:
  0.0 50.9 jit_solution(15243825888707057524)
XLA Ops:
  0.7 1.1 %shard_map.114 = (bf16[4,64,384]{2,1,0:T(8,128)(2,1)S(1)}, bf16[3,2,64,384]{3,2,1,0:T(8,128)(2,1)S(1)}) custom-call(bf16[2,2,64,384]{3,2,1,0:T(8,128)(2,1)} %latents_ref.1, bf16[2,2,64,384]{3,2,1,0:T(8,128)(2,1)} %cache_ref.1), custom_call_target="tpu_custom_call" | custom-call | bytes 491520 | tf_op jit(solution)/shard_map/pallas_call | solution.py:467
  1.8 3.7 %collective-permute-start = (bf16[4,64,384]{2,1,0:T(8,128)(2,1)S(1)}, bf16[4,64,384]{2,1,0:T(8,128)(2,1)S(1)}, u32[]{:S(2)}, u32[]{:S(2)}) collective-permute-start(bf16[4,64,384]{2,1,0:T(8,128)(2,1)S(1)} %get-tuple-element.31), channel_id=1, source_target_pairs={{1,2},{3,4},{5,6},{7,8},{9,10},{11,12},{13,14},{2,1},{4,3},{6,5},{... | collective-permute-start | bytes 589832 | tf_op jit(solution)/shard_map/ppermute | solution.py:479
  5.6 3.8 %shard_map.115 = (bf16[2,128,384]{2,1,0:T(8,128)(2,1)}, bf16[3,128,384]{2,1,0:T(8,128)(2,1)S(1)}, bf16[3,3,384,1152]{3,2,1,0:T(8,128)(2,1)S(1)}) custom-call(bf16[2,128,384]{2,1,0:T(8,128)(2,1)} %bitcast.8, bf16[2,128,384]{2,1,0:T(8,128)(2,1)} %bitcast.9, bf16[3,3,3,384,384]{4,3,2,1,0:T(8,128)(2,1)} %weight_ref.1, f32[384]{0:T(512)} %norm_gain_ref.1), custom_call_target="tpu_custom_call" | custom-call | flops 983040 | bytes 7962624 | tf_op jit(solution)/shard_map/pallas_call | solution.py:481
  9.4 1.5 %collective-permute-done.edge_ref = bf16[4,64,384]{2,1,0:T(8,128)(2,1)S(1)} collective-permute-done((bf16[4,64,384]{2,1,0:T(8,128)(2,1)S(1)}, bf16[4,64,384]{2,1,0:T(8,128)(2,1)S(1)}, u32[]{:S(2)}, u32[]{:S(2)}) %collective-permute-start) | collective-permute-done | bytes 196640 | tf_op jit(solution)/shard_map/ppermute | solution.py:479
  11.0 1.4 %collective-permute-done.2.far_ref = bf16[4,64,384]{2,1,0:T(8,128)(2,1)S(1)} collective-permute-done((bf16[4,64,384]{2,1,0:T(8,128)(2,1)S(1)}, bf16[4,64,384]{2,1,0:T(8,128)(2,1)S(1)}, u32[]{:S(2)}, u32[]{:S(2)}) %collective-permute-start.2) | collective-permute-done | bytes 196640 | tf_op jit(solution)/shard_map/ppermute | solution.py:507
  12.4 3.1 %shard_map.116 = (bf16[272,384]{1,0:T(8,128)(2,1)S(1)}, bf16[144,384]{1,0:T(8,128)(2,1)S(1)}, bf16[144,384]{1,0:T(8,128)(2,1)S(1)}, f32[256,384]{1,0:T(8,128)S(1)}) custom-call(bf16[3,128,384]{2,1,0:T(8,128)(2,1)S(1)} %get-tuple-element.33.own_ref, bf16[3,128,384]{2,1,0:T(8,128)(2,1)S(1)} %bitcast.6, bf16[4,64,384]{2,1,0:T(8,128)(2,1)S(1)} %collective-permute-done.edge_ref, ...), custom_call_target="tpu_custom_call" | custom-call | flops 2038431744 | bytes 7962624 | tf_op jit(solution)/shard_map/pallas_call | solution.py:510
  15.5 0.2 collective-permute-start.3
  15.7 1.5 %collective-permute-start.5 = (bf16[272,384]{1,0:T(8,128)(2,1)S(1)}, bf16[272,384]{1,0:T(8,128)(2,1)S(1)}, u32[]{:S(2)}, u32[]{:S(2)}) collective-permute-start(bf16[272,384]{1,0:T(8,128)(2,1)S(1)} %get-tuple-element.53.refs_0_), channel_id=1, source_target_pairs={{0,2},{1,3},{2,0},{3,1},{4,6},{5,7},{6,4},{7,5},{8,10},{9,11},{10,... | collective-permute-start | bytes 626696 | tf_op jit(solution)/shard_map/ppermute | solution.py:394
  17.3 3.7 %collective-permute-done.3.refs_1_ = bf16[144,384]{1,0:T(8,128)(2,1)S(1)} collective-permute-done((bf16[144,384]{1,0:T(8,128)(2,1)S(1)}, bf16[144,384]{1,0:T(8,128)(2,1)S(1)}, u32[]{:S(2)}, u32[]{:S(2)}) %collective-permute-start.3) | collective-permute-done | bytes 110624 | tf_op jit(solution)/shard_map/ppermute | solution.py:394
  21.0 0.5 collective-permute-start.7
  21.5 1.7 %collective-permute-done.4.refs_2_ = bf16[144,384]{1,0:T(8,128)(2,1)S(1)} collective-permute-done((bf16[144,384]{1,0:T(8,128)(2,1)S(1)}, bf16[144,384]{1,0:T(8,128)(2,1)S(1)}, u32[]{:S(2)}, u32[]{:S(2)}) %collective-permute-start.4) | collective-permute-done | bytes 110624 | tf_op jit(solution)/shard_map/ppermute | solution.py:394
  23.2 0.7 %collective-permute-start.9 = (bf16[144,384]{1,0:T(8,128)(2,1)S(1)}, bf16[144,384]{1,0:T(8,128)(2,1)S(1)}, u32[]{:S(2)}, u32[]{:S(2)}) collective-permute-start(bf16[144,384]{1,0:T(8,128)(2,1)S(1)} %collective-permute-done.4.refs_2_), channel_id=1, source_target_pairs={{0,2},{1,3},{2,0},{3,1},{4,6},{5,7},{6,4},{7,5},{8,10},{9,11},{10,... | collective-permute-start | bytes 331784 | tf_op jit(solution)/shard_map/ppermute | solution.py:394
  23.8 1.8 %collective-permute-start.12 = (bf16[272,384]{1,0:T(8,128)(2,1)S(1)}, bf16[272,384]{1,0:T(8,128)(2,1)S(1)}, u32[]{:S(2)}, u32[]{:S(2)}) collective-permute-start(bf16[272,384]{1,0:T(8,128)(2,1)S(1)} %get-tuple-element.53.refs_0_), channel_id=1, source_target_pairs={{0,8},{1,9},{2,10},{3,11},{4,0},{5,1},{6,2},{7,3},{8,12},{9,13},{1... | collective-permute-start | bytes 626696 | tf_op jit(solution)/shard_map/ppermute | solution.py:394
  25.6 1.3 %collective-permute-start.13 = (bf16[272,384]{1,0:T(8,128)(2,1)S(1)}, bf16[272,384]{1,0:T(8,128)(2,1)S(1)}, u32[]{:S(2)}, u32[]{:S(2)}) collective-permute-start(bf16[272,384]{1,0:T(8,128)(2,1)S(1)} %collective-permute-done.5.refs_7_), channel_id=1, source_target_pairs={{0,8},{1,9},{2,10},{3,11},{4,0},{5,1},{6,2},{7,3},{8,12},{9,13},{1... | collective-permute-start | bytes 626696 | tf_op jit(solution)/shard_map/ppermute | solution.py:394
  26.9 0.2 collective-permute-start.10
  27.2 3.3 %collective-permute-done.8.refs_6_ = bf16[144,384]{1,0:T(8,128)(2,1)S(1)} collective-permute-done((bf16[144,384]{1,0:T(8,128)(2,1)S(1)}, bf16[144,384]{1,0:T(8,128)(2,1)S(1)}, u32[]{:S(2)}, u32[]{:S(2)}) %collective-permute-start.8) | collective-permute-done | bytes 110624 | tf_op jit(solution)/shard_map/ppermute | solution.py:394
  30.5 0.5 %shard_map.113 = (bf16[384,384]{1,0:T(8,128)(2,1)S(1)}, bf16[384,384]{1,0:T(8,128)(2,1)S(1)}) custom-call(bf16[384,384]{1,0:T(8,128)(2,1)S(1)} %copy-done, bf16[384,384]{1,0:T(8,128)(2,1)S(1)} %copy-done.1, bf16[384,384]{1,0:T(8,128)(2,1)S(1)} %copy-done.2, bf16[384,384]{1,0:T(8,128)(2,1)S(1)} %copy-done.3), custom_call_target="tpu_custom_call" | custom-call | flops 226492416 | bytes 1769472 | tf_op jit(solution)/shard_map/pallas_call | solution.py:542
  31.0 1.4 %shard_map.117 = (bf16[256,384]{1,0:T(8,128)(2,1)S(1)}, f32[256,128]{1,0:T(8,128)S(1)}, f32[256,128]{1,0:T(8,128)S(1)}, f32[256,384]{1,0:T(8,128)S(1)}) custom-call(bf16[384,384]{1,0:T(8,128)(2,1)S(1)} %get-tuple-element.30.score_ref, bf16[272,384]{1,0:T(8,128)(2,1)S(1)} %get-tuple-element.53.refs_0_, bf16[144,384]{1,0:T(8,128)(2,1)S(1)} %collective-permute-done.3.refs_1_, ...), custom_call_target="tpu_custom_call" | custom-call | flops 503316480 | bytes 983040 | tf_op jit(solution)/shard_map/pallas_call | solution.py:553
  32.5 0.6 %collective-permute-done.12.refs_10_ = bf16[272,384]{1,0:T(8,128)(2,1)S(1)} collective-permute-done((bf16[272,384]{1,0:T(8,128)(2,1)S(1)}, bf16[272,384]{1,0:T(8,128)(2,1)S(1)}, u32[]{:S(2)}, u32[]{:S(2)}) %collective-permute-start.12) | collective-permute-done | bytes 208928 | tf_op jit(solution)/shard_map/ppermute | solution.py:394
  33.1 4.5 %collective-permute-done.13.refs_11_ = bf16[272,384]{1,0:T(8,128)(2,1)S(1)} collective-permute-done((bf16[272,384]{1,0:T(8,128)(2,1)S(1)}, bf16[272,384]{1,0:T(8,128)(2,1)S(1)}, u32[]{:S(2)}, u32[]{:S(2)}) %collective-permute-start.13) | collective-permute-done | bytes 208928 | tf_op jit(solution)/shard_map/ppermute | solution.py:394
  37.5 2.6 %shard_map.118 = (bf16[256,384]{1,0:T(8,128)(2,1)S(1)}, bf16[256,384]{1,0:T(8,128)(2,1)S(1)}) custom-call(bf16[256,384]{1,0:T(8,128)(2,1)S(1)} %get-tuple-element.47.own_query_ref, f32[256,128]{1,0:T(8,128)S(1)} %get-tuple-element.48.peak_ref, f32[256,128]{1,0:T(8,128)S(1)} %get-tuple-element.49.sums_ref, f32[256,384]{1,0:T(8,128)S(1)} %get-tuple-element.50.added_ref, ...), custom_call_target="tpu_custom_call" | custom-call | flops 603979776 | bytes 1572864 | tf_op jit(solution)/shard_map/pallas_call | solution.py:572
  40.1 6.7 %collective-permute-start.14 = (bf16[256,384]{1,0:T(8,128)(2,1)S(1)}, bf16[256,384]{1,0:T(8,128)(2,1)S(1)}, u32[]{:S(2)}, u32[]{:S(2)}) collective-permute-start(bf16[256,384]{1,0:T(8,128)(2,1)S(1)} %get-tuple-element.56), channel_id=1, source_target_pairs={{0,1},{1,0},{2,3},{3,2},{4,5},{5,4},{6,7},{7,6},{8,9},{9,8},{10,11... | collective-permute-start | bytes 589832 | tf_op jit(solution)/shard_map/ppermute | solution.py:601
  46.9 1.1 %collective-permute-done.14.swap_ref = bf16[256,384]{1,0:T(8,128)(2,1)S(1)} collective-permute-done((bf16[256,384]{1,0:T(8,128)(2,1)S(1)}, bf16[256,384]{1,0:T(8,128)(2,1)S(1)}, u32[]{:S(2)}, u32[]{:S(2)}) %collective-permute-start.14) | collective-permute-done | bytes 196640 | tf_op jit(solution)/shard_map/ppermute | solution.py:601
  47.9 3.0 %shard_map.119 = bf16[2,4,192,128]{3,2,1,0:T(8,128)(2,1)} custom-call(bf16[256,384]{1,0:T(8,128)(2,1)S(1)} %get-tuple-element.55.mid_ref, bf16[256,384]{1,0:T(8,128)(2,1)S(1)} %collective-permute-done.14.swap_ref, bf16[3,3,192,384]{3,2,1,0:T(8,128)(2,1)S(1)} %bitcast.7), custom_call_target="tpu_custom_call" | custom-call | flops 1358954496 | bytes 1327104 | tf_op jit(solution)/shard_map/pallas_call | solution.py:604
  (27 shorter events, 0.2 us)
Async XLA Ops:
  0.6 11.8 %copy-start.4 = (f32[384]{0:T(512)S(1)}, f32[384]{0:T(512)}, u32[]{:S(2)}) copy-start(f32[384]{0:T(512)} %norm_gain_ref.1) | copy-start | bytes 4612
  0.6 11.8 %copy-start.5 = (f32[384]{0:T(512)S(1)}, f32[384]{0:T(512)}, u32[]{:S(2)}) copy-start(f32[384]{0:T(512)} %gain_ref.3) | copy-start | bytes 4612
  1.8 9.2 %collective-permute-start = (bf16[4,64,384]{2,1,0:T(8,128)(2,1)S(1)}, bf16[4,64,384]{2,1,0:T(8,128)(2,1)S(1)}, u32[]{:S(2)}, u32[]{:S(2)}) collective-permute-start(bf16[4,64,384]{2,1,0:T(8,128)(2,1)S(1)} %get-tuple-element.31), channel_id=1, source_target_pairs={{1,2},{3,4},{5,6},{7,8},{9,10},{11,12},{13,14},{2,1},{4,3},{6,5},{... | collective-permute-start | bytes 589832 | tf_op jit(solution)/shard_map/ppermute | solution.py:479
  5.5 5.5 %collective-permute-start.1 = (bf16[3,2,64,384]{3,2,1,0:T(8,128)(2,1)S(1)}, bf16[3,2,64,384]{3,2,1,0:T(8,128)(2,1)S(1)}, u32[]{:S(2)}, u32[]{:S(2)}) collective-permute-start(bf16[3,2,64,384]{3,2,1,0:T(8,128)(2,1)S(1)} %get-tuple-element.34), channel_id=1, source_target_pairs={{0,1},{1,0},{2,3},{3,2},{4,5},{5,4},{6,7},{7,6},{8,9},{9,8},{10,11... | collective-permute-start | bytes 884744 | tf_op jit(solution)/shard_map/ppermute | solution.py:480
  5.6 24.8 %copy-start = (bf16[384,384]{1,0:T(8,128)(2,1)S(1)}, bf16[384,384]{1,0:T(8,128)(2,1)}, u32[]{:S(2)}) copy-start(bf16[384,384]{1,0:T(8,128)(2,1)} %query_ref.1) | copy-start | bytes 884740
  5.6 24.8 %copy-start.1 = (bf16[384,384]{1,0:T(8,128)(2,1)S(1)}, bf16[384,384]{1,0:T(8,128)(2,1)}, u32[]{:S(2)}) copy-start(bf16[384,384]{1,0:T(8,128)(2,1)} %key_ref.1) | copy-start | bytes 884740
  5.6 24.8 %copy-start.2 = (bf16[384,384]{1,0:T(8,128)(2,1)S(1)}, bf16[384,384]{1,0:T(8,128)(2,1)}, u32[]{:S(2)}) copy-start(bf16[384,384]{1,0:T(8,128)(2,1)} %value_ref.1) | copy-start | bytes 884740
  5.6 24.8 %copy-start.3 = (bf16[384,384]{1,0:T(8,128)(2,1)S(1)}, bf16[384,384]{1,0:T(8,128)(2,1)}, u32[]{:S(2)}) copy-start(bf16[384,384]{1,0:T(8,128)(2,1)} %out_ref.1) | copy-start | bytes 884740
  9.4 38.5 %copy-start.6 = (bf16[3,3,384,192]{2,3,1,0:T(8,128)(2,1)S(1)}, bf16[3,3,384,192]{2,3,1,0:T(8,128)(2,1)}, u32[]{:S(2)}) copy-start(bf16[3,3,384,192]{2,3,1,0:T(8,128)(2,1)} %param.19) | copy-start | bytes 3981316
  11.0 1.4 %collective-permute-start.2 = (bf16[4,64,384]{2,1,0:T(8,128)(2,1)S(1)}, bf16[4,64,384]{2,1,0:T(8,128)(2,1)S(1)}, u32[]{:S(2)}, u32[]{:S(2)}) collective-permute-start(bf16[4,64,384]{2,1,0:T(8,128)(2,1)S(1)} %collective-permute-done.edge_ref), channel_id=1, source_target_pairs={{0,1},{1,0},{2,3},{3,2},{4,5},{5,4},{6,7},{7,6},{8,9},{9,8},{10,11... | collective-permute-start | bytes 589832 | tf_op jit(solution)/shard_map/ppermute | solution.py:507
  15.5 5.5 %collective-permute-start.3 = (bf16[144,384]{1,0:T(8,128)(2,1)S(1)}, bf16[144,384]{1,0:T(8,128)(2,1)S(1)}, u32[]{:S(2)}, u32[]{:S(2)}) collective-permute-start(bf16[144,384]{1,0:T(8,128)(2,1)S(1)} %get-tuple-element.38), channel_id=1, source_target_pairs={{0,4},{1,5},{2,6},{3,7},{4,12},{5,13},{6,14},{7,15},{8,0},{9,1},{1... | collective-permute-start | bytes 331784 | tf_op jit(solution)/shard_map/ppermute | solution.py:394
  15.7 7.4 %collective-permute-start.5 = (bf16[272,384]{1,0:T(8,128)(2,1)S(1)}, bf16[272,384]{1,0:T(8,128)(2,1)S(1)}, u32[]{:S(2)}, u32[]{:S(2)}) collective-permute-start(bf16[272,384]{1,0:T(8,128)(2,1)S(1)} %get-tuple-element.53.refs_0_), channel_id=1, source_target_pairs={{0,2},{1,3},{2,0},{3,1},{4,6},{5,7},{6,4},{7,5},{8,10},{9,11},{10,... | collective-permute-start | bytes 626696 | tf_op jit(solution)/shard_map/ppermute | solution.py:394
  17.2 6.0 %collective-permute-start.4 = (bf16[144,384]{1,0:T(8,128)(2,1)S(1)}, bf16[144,384]{1,0:T(8,128)(2,1)S(1)}, u32[]{:S(2)}, u32[]{:S(2)}) collective-permute-start(bf16[144,384]{1,0:T(8,128)(2,1)S(1)} %get-tuple-element.39), channel_id=1, source_target_pairs={{0,4},{1,5},{2,6},{3,7},{4,12},{5,13},{6,14},{7,15},{8,0},{9,1},{1... | collective-permute-start | bytes 331784 | tf_op jit(solution)/shard_map/ppermute | solution.py:394
  21.0 4.7 %collective-permute-start.6 = (bf16[144,384]{1,0:T(8,128)(2,1)S(1)}, bf16[144,384]{1,0:T(8,128)(2,1)S(1)}, u32[]{:S(2)}, u32[]{:S(2)}) collective-permute-start(bf16[144,384]{1,0:T(8,128)(2,1)S(1)} %collective-permute-done.3.refs_1_), channel_id=1, source_target_pairs={{0,4},{1,5},{2,6},{3,7},{4,12},{5,13},{6,14},{7,15},{8,0},{9,1},{1... | collective-permute-start | bytes 331784 | tf_op jit(solution)/shard_map/ppermute | solution.py:394
  21.0 4.7 %collective-permute-start.7 = (bf16[144,384]{1,0:T(8,128)(2,1)S(1)}, bf16[144,384]{1,0:T(8,128)(2,1)S(1)}, u32[]{:S(2)}, u32[]{:S(2)}) collective-permute-start(bf16[144,384]{1,0:T(8,128)(2,1)S(1)} %collective-permute-done.3.refs_1_), channel_id=1, source_target_pairs={{0,2},{1,3},{2,0},{3,1},{4,6},{5,7},{6,4},{7,5},{8,10},{9,11},{10,... | collective-permute-start | bytes 331784 | tf_op jit(solution)/shard_map/ppermute | solution.py:394
  23.2 7.3 %collective-permute-start.8 = (bf16[144,384]{1,0:T(8,128)(2,1)S(1)}, bf16[144,384]{1,0:T(8,128)(2,1)S(1)}, u32[]{:S(2)}, u32[]{:S(2)}) collective-permute-start(bf16[144,384]{1,0:T(8,128)(2,1)S(1)} %collective-permute-done.4.refs_2_), channel_id=1, source_target_pairs={{0,4},{1,5},{2,6},{3,7},{4,12},{5,13},{6,14},{7,15},{8,0},{9,1},{1... | collective-permute-start | bytes 331784 | tf_op jit(solution)/shard_map/ppermute | solution.py:394
  23.2 7.3 %collective-permute-start.9 = (bf16[144,384]{1,0:T(8,128)(2,1)S(1)}, bf16[144,384]{1,0:T(8,128)(2,1)S(1)}, u32[]{:S(2)}, u32[]{:S(2)}) collective-permute-start(bf16[144,384]{1,0:T(8,128)(2,1)S(1)} %collective-permute-done.4.refs_2_), channel_id=1, source_target_pairs={{0,2},{1,3},{2,0},{3,1},{4,6},{5,7},{6,4},{7,5},{8,10},{9,11},{10,... | collective-permute-start | bytes 331784 | tf_op jit(solution)/shard_map/ppermute | solution.py:394
  23.8 9.2 %collective-permute-start.12 = (bf16[272,384]{1,0:T(8,128)(2,1)S(1)}, bf16[272,384]{1,0:T(8,128)(2,1)S(1)}, u32[]{:S(2)}, u32[]{:S(2)}) collective-permute-start(bf16[272,384]{1,0:T(8,128)(2,1)S(1)} %get-tuple-element.53.refs_0_), channel_id=1, source_target_pairs={{0,8},{1,9},{2,10},{3,11},{4,0},{5,1},{6,2},{7,3},{8,12},{9,13},{1... | collective-permute-start | bytes 626696 | tf_op jit(solution)/shard_map/ppermute | solution.py:394
  25.6 11.9 %collective-permute-start.13 = (bf16[272,384]{1,0:T(8,128)(2,1)S(1)}, bf16[272,384]{1,0:T(8,128)(2,1)S(1)}, u32[]{:S(2)}, u32[]{:S(2)}) collective-permute-start(bf16[272,384]{1,0:T(8,128)(2,1)S(1)} %collective-permute-done.5.refs_7_), channel_id=1, source_target_pairs={{0,8},{1,9},{2,10},{3,11},{4,0},{5,1},{6,2},{7,3},{8,12},{9,13},{1... | collective-permute-start | bytes 626696 | tf_op jit(solution)/shard_map/ppermute | solution.py:394
  26.9 5.5 %collective-permute-start.10 = (bf16[144,384]{1,0:T(8,128)(2,1)S(1)}, bf16[144,384]{1,0:T(8,128)(2,1)S(1)}, u32[]{:S(2)}, u32[]{:S(2)}) collective-permute-start(bf16[144,384]{1,0:T(8,128)(2,1)S(1)} %collective-permute-done.6.refs_5_), channel_id=1, source_target_pairs={{0,2},{1,3},{2,0},{3,1},{4,6},{5,7},{6,4},{7,5},{8,10},{9,11},{10,... | collective-permute-start | bytes 331784 | tf_op jit(solution)/shard_map/ppermute | solution.py:394
  30.4 7.1 %collective-permute-start.11 = (bf16[144,384]{1,0:T(8,128)(2,1)S(1)}, bf16[144,384]{1,0:T(8,128)(2,1)S(1)}, u32[]{:S(2)}, u32[]{:S(2)}) collective-permute-start(bf16[144,384]{1,0:T(8,128)(2,1)S(1)} %collective-permute-done.8.refs_6_), channel_id=1, source_target_pairs={{0,2},{1,3},{2,0},{3,1},{4,6},{5,7},{6,4},{7,5},{8,10},{9,11},{10,... | collective-permute-start | bytes 331784 | tf_op jit(solution)/shard_map/ppermute | solution.py:394
  40.1 7.8 %collective-permute-start.14 = (bf16[256,384]{1,0:T(8,128)(2,1)S(1)}, bf16[256,384]{1,0:T(8,128)(2,1)S(1)}, u32[]{:S(2)}, u32[]{:S(2)}) collective-permute-start(bf16[256,384]{1,0:T(8,128)(2,1)S(1)} %get-tuple-element.56), channel_id=1, source_target_pairs={{0,1},{1,0},{2,3},{3,2},{4,5},{5,4},{6,7},{7,6},{8,9},{9,8},{10,11... | collective-permute-start | bytes 589832 | tf_op jit(solution)/shard_map/ppermute | solution.py:601
where the time goes:
time: 51.1 us; the launch traced here: 50.9 us
  waiting for transfers between devices  17.8 us (35%)
  starting transfers between devices  16.8 us (33%)
  Pallas kernels  15.5 us (30%)
  between operations  0.79 us (2%)
    ppermute x11, waiting for transfers between devices, send(): return [lax.ppermute(part, 'rows', pairs) for part in parts]  13.7 us
    ppermute x1, starting transfers between devices, shards(): swap_rows = lax.ppermute(swap_rows, 'rows', swap)  6.73 us
    ppermute x11, starting transfers between devices, send(): return [lax.ppermute(part, 'rows', pairs) for part in parts]  6.26 us
    pallas_call x1, Pallas kernels, shards(): pl.pallas_call(prepare_kernel, out_shape=(jax.ShapeDtypeStruct((frames, o...  3.76 us
    ppermute x1, starting transfers between devices, shards(): edge_rows = lax.ppermute(edge_rows, 'rows', neighbour)  3.71 us
    pallas_call x1, Pallas kernels, shards(): pl.pallas_call(functools.partial(conv_kernel, width), out_shape=(block, h...  3.08 us
    pallas_call x1, Pallas kernels, shards(): pl.pallas_call(functools.partial(up_kernel, width), out_shape=jax.ShapeDt...  2.98 us
    pallas_call x1, Pallas kernels, shards(): pl.pallas_call(functools.partial(late_kernel, width, sources, counts, len...  2.59 us
  transfers between devices with their start and end apart: 15, of which 8 were waited for; matrix products, arithmetic and copies ran while one was open for 0% of the time, Pallas kernels for 11%

commit v1 on v0

--- a/solution.py
+++ b/solution.py
@@ -431,7 +431,7 @@
         if length > 1:
             if steps > 0:
                 crossed = list(crossed)
-                tie((crossed, 0), (parts, 0))
+                tie((crossed, 0), (parts, 1))
             late.append((send(crossed, backward), moved(moved(here, across), backward)))
     return early, late
 

time: 51.1 us -> 55.2 us (1.080)
  the two profiles are of different devices: /device:TPU:25 before, /device:TPU:1 now
where the time goes in v1:
time: 55.2 us; the launch traced here: 54.7 us
  starting transfers between devices  23.7 us (43%)
  Pallas kernels  15.5 us (28%)
  waiting for transfers between devices  14.8 us (27%)
  between operations  0.76 us (1%)
    ppermute x11, starting transfers between devices, send(): return [lax.ppermute(part, 'rows', pairs) for part in parts]  11.9 us
    ppermute x11, waiting for transfers between devices, send(): return [lax.ppermute(part, 'rows', pairs) for part in parts]  11.5 us
    ppermute x1, starting transfers between devices, shards(): swap_rows = lax.ppermute(swap_rows, 'rows', swap)  7.14 us
    ppermute x1, starting transfers between devices, shards(): edge_rows = lax.ppermute(edge_rows, 'rows', neighbour)  4.54 us
    pallas_call x1, Pallas kernels, shards(): pl.pallas_call(prepare_kernel, out_shape=(jax.ShapeDtypeStruct((frames, o...  3.76 us
    pallas_call x1, Pallas kernels, shards(): pl.pallas_call(functools.partial(conv_kernel, width), out_shape=(block, h...  3.08 us
    pallas_call x1, Pallas kernels, shards(): pl.pallas_call(functools.partial(up_kernel, width), out_shape=jax.ShapeDt...  2.98 us
    pallas_call x1, Pallas kernels, shards(): pl.pallas_call(functools.partial(late_kernel, width, sources, counts, len...  2.57 us
  transfers between devices with their start and end apart: 15, of which 11 were waited for; matrix products, arithmetic and copies ran while one was open for 0% of the time, Pallas kernels for 10%

profile of v1, /device:TPU:1, one launch (start us, length us, event | category | flops | bytes accessed | tf_op | source)
XLA Modules:
  0.0 54.7 jit_solution(3988839444452626139)
XLA Ops:
  0.7 1.1 %shard_map.114 = (bf16[4,64,384]{2,1,0:T(8,128)(2,1)S(1)}, bf16[3,2,64,384]{3,2,1,0:T(8,128)(2,1)S(1)}) custom-call(bf16[2,2,64,384]{3,2,1,0:T(8,128)(2,1)} %latents_ref.1, bf16[2,2,64,384]{3,2,1,0:T(8,128)(2,1)} %cache_ref.1), custom_call_target="tpu_custom_call" | custom-call | bytes 491520 | tf_op jit(solution)/shard_map/pallas_call | solution.py:467
  1.8 4.5 %collective-permute-start = (bf16[4,64,384]{2,1,0:T(8,128)(2,1)S(1)}, bf16[4,64,384]{2,1,0:T(8,128)(2,1)S(1)}, u32[]{:S(2)}, u32[]{:S(2)}) collective-permute-start(bf16[4,64,384]{2,1,0:T(8,128)(2,1)S(1)} %get-tuple-element.31), channel_id=1, source_target_pairs={{1,2},{3,4},{5,6},{7,8},{9,10},{11,12},{13,14},{2,1},{4,3},{6,5},{... | collective-permute-start | bytes 589832 | tf_op jit(solution)/shard_map/ppermute | solution.py:479
  6.5 3.8 %shard_map.115 = (bf16[2,128,384]{2,1,0:T(8,128)(2,1)}, bf16[3,128,384]{2,1,0:T(8,128)(2,1)S(1)}, bf16[3,3,384,1152]{3,2,1,0:T(8,128)(2,1)S(1)}) custom-call(bf16[2,128,384]{2,1,0:T(8,128)(2,1)} %bitcast.8, bf16[2,128,384]{2,1,0:T(8,128)(2,1)} %bitcast.9, bf16[3,3,3,384,384]{4,3,2,1,0:T(8,128)(2,1)} %weight_ref.1, f32[384]{0:T(512)} %norm_gain_ref.1), custom_call_target="tpu_custom_call" | custom-call | flops 983040 | bytes 7962624 | tf_op jit(solution)/shard_map/pallas_call | solution.py:481
  10.3 0.8 %collective-permute-done.edge_ref = bf16[4,64,384]{2,1,0:T(8,128)(2,1)S(1)} collective-permute-done((bf16[4,64,384]{2,1,0:T(8,128)(2,1)S(1)}, bf16[4,64,384]{2,1,0:T(8,128)(2,1)S(1)}, u32[]{:S(2)}, u32[]{:S(2)}) %collective-permute-start) | collective-permute-done | bytes 196640 | tf_op jit(solution)/shard_map/ppermute | solution.py:479
  11.1 1.4 %collective-permute-done.2.far_ref = bf16[4,64,384]{2,1,0:T(8,128)(2,1)S(1)} collective-permute-done((bf16[4,64,384]{2,1,0:T(8,128)(2,1)S(1)}, bf16[4,64,384]{2,1,0:T(8,128)(2,1)S(1)}, u32[]{:S(2)}, u32[]{:S(2)}) %collective-permute-start.2) | collective-permute-done | bytes 196640 | tf_op jit(solution)/shard_map/ppermute | solution.py:507
  12.5 3.1 %shard_map.116 = (bf16[272,384]{1,0:T(8,128)(2,1)S(1)}, bf16[144,384]{1,0:T(8,128)(2,1)S(1)}, bf16[144,384]{1,0:T(8,128)(2,1)S(1)}, f32[256,384]{1,0:T(8,128)S(1)}) custom-call(bf16[3,128,384]{2,1,0:T(8,128)(2,1)S(1)} %get-tuple-element.33.own_ref, bf16[3,128,384]{2,1,0:T(8,128)(2,1)S(1)} %bitcast.6, bf16[4,64,384]{2,1,0:T(8,128)(2,1)S(1)} %collective-permute-done.edge_ref, ...), custom_call_target="tpu_custom_call" | custom-call | flops 2038431744 | bytes 7962624 | tf_op jit(solution)/shard_map/pallas_call | solution.py:510
  15.6 2.3 %collective-permute-start.5 = (bf16[272,384]{1,0:T(8,128)(2,1)S(1)}, bf16[272,384]{1,0:T(8,128)(2,1)S(1)}, u32[]{:S(2)}, u32[]{:S(2)}) collective-permute-start(bf16[272,384]{1,0:T(8,128)(2,1)S(1)} %get-tuple-element.53.refs_0_), channel_id=1, source_target_pairs={{0,2},{1,3},{2,0},{3,1},{4,6},{5,7},{6,4},{7,5},{8,10},{9,11},{10,... | collective-permute-start | bytes 626696 | tf_op jit(solution)/shard_map/ppermute | solution.py:394
  17.9 1.3 %collective-permute-start.4 = (bf16[144,384]{1,0:T(8,128)(2,1)S(1)}, bf16[144,384]{1,0:T(8,128)(2,1)S(1)}, u32[]{:S(2)}, u32[]{:S(2)}) collective-permute-start(bf16[144,384]{1,0:T(8,128)(2,1)S(1)} %get-tuple-element.39), channel_id=1, source_target_pairs={{0,4},{1,5},{2,6},{3,7},{4,12},{5,13},{6,14},{7,15},{8,0},{9,1},{1... | collective-permute-start | bytes 331784 | tf_op jit(solution)/shard_map/ppermute | solution.py:394
  19.2 0.9 %collective-permute-start.3 = (bf16[144,384]{1,0:T(8,128)(2,1)S(1)}, bf16[144,384]{1,0:T(8,128)(2,1)S(1)}, u32[]{:S(2)}, u32[]{:S(2)}) collective-permute-start(bf16[144,384]{1,0:T(8,128)(2,1)S(1)} %get-tuple-element.38), channel_id=1, source_target_pairs={{0,4},{1,5},{2,6},{3,7},{4,12},{5,13},{6,14},{7,15},{8,0},{9,1},{1... | collective-permute-start | bytes 331784 | tf_op jit(solution)/shard_map/ppermute | solution.py:394
  20.1 2.7 %collective-permute-done.4.refs_2_ = bf16[144,384]{1,0:T(8,128)(2,1)S(1)} collective-permute-done((bf16[144,384]{1,0:T(8,128)(2,1)S(1)}, bf16[144,384]{1,0:T(8,128)(2,1)S(1)}, u32[]{:S(2)}, u32[]{:S(2)}) %collective-permute-start.4) | collective-permute-done | bytes 110624 | tf_op jit(solution)/shard_map/ppermute | solution.py:394
  23.1 1.2 %collective-permute-start.8 = (bf16[144,384]{1,0:T(8,128)(2,1)S(1)}, bf16[144,384]{1,0:T(8,128)(2,1)S(1)}, u32[]{:S(2)}, u32[]{:S(2)}) collective-permute-start(bf16[144,384]{1,0:T(8,128)(2,1)S(1)} %collective-permute-done.4.refs_2_), channel_id=1, source_target_pairs={{0,4},{1,5},{2,6},{3,7},{4,12},{5,13},{6,14},{7,15},{8,0},{9,1},{1... | collective-permute-start | bytes 331784 | tf_op jit(solution)/shard_map/ppermute | solution.py:394
  24.4 1.2 %collective-permute-start.9 = (bf16[144,384]{1,0:T(8,128)(2,1)S(1)}, bf16[144,384]{1,0:T(8,128)(2,1)S(1)}, u32[]{:S(2)}, u32[]{:S(2)}) collective-permute-start(bf16[144,384]{1,0:T(8,128)(2,1)S(1)} %collective-permute-done.4.refs_2_), channel_id=1, source_target_pairs={{0,2},{1,3},{2,0},{3,1},{4,6},{5,7},{6,4},{7,5},{8,10},{9,11},{10,... | collective-permute-start | bytes 331784 | tf_op jit(solution)/shard_map/ppermute | solution.py:394
  25.6 1.3 %collective-permute-start.6 = (bf16[144,384]{1,0:T(8,128)(2,1)S(1)}, bf16[144,384]{1,0:T(8,128)(2,1)S(1)}, u32[]{:S(2)}, u32[]{:S(2)}) collective-permute-start(bf16[144,384]{1,0:T(8,128)(2,1)S(1)} %collective-permute-done.3.refs_1_), channel_id=1, source_target_pairs={{0,4},{1,5},{2,6},{3,7},{4,12},{5,13},{6,14},{7,15},{8,0},{9,1},{1... | collective-permute-start | bytes 331784 | tf_op jit(solution)/shard_map/ppermute | solution.py:394
  26.9 1.2 %collective-permute-start.7 = (bf16[144,384]{1,0:T(8,128)(2,1)S(1)}, bf16[144,384]{1,0:T(8,128)(2,1)S(1)}, u32[]{:S(2)}, u32[]{:S(2)}) collective-permute-start(bf16[144,384]{1,0:T(8,128)(2,1)S(1)} %collective-permute-done.3.refs_1_), channel_id=1, source_target_pairs={{0,2},{1,3},{2,0},{3,1},{4,6},{5,7},{6,4},{7,5},{8,10},{9,11},{10,... | collective-permute-start | bytes 331784 | tf_op jit(solution)/shard_map/ppermute | solution.py:394
  28.2 0.9 %collective-permute-start.13 = (bf16[272,384]{1,0:T(8,128)(2,1)S(1)}, bf16[272,384]{1,0:T(8,128)(2,1)S(1)}, u32[]{:S(2)}, u32[]{:S(2)}) collective-permute-start(bf16[272,384]{1,0:T(8,128)(2,1)S(1)} %collective-permute-done.5.refs_7_), channel_id=1, source_target_pairs={{0,8},{1,9},{2,10},{3,11},{4,0},{5,1},{6,2},{7,3},{8,12},{9,13},{1... | collective-permute-start | bytes 626696 | tf_op jit(solution)/shard_map/ppermute | solution.py:394
  29.1 2.2 %collective-permute-done.6.refs_5_ = bf16[144,384]{1,0:T(8,128)(2,1)S(1)} collective-permute-done((bf16[144,384]{1,0:T(8,128)(2,1)S(1)}, bf16[144,384]{1,0:T(8,128)(2,1)S(1)}, u32[]{:S(2)}, u32[]{:S(2)}) %collective-permute-start.6) | collective-permute-done | bytes 110624 | tf_op jit(solution)/shard_map/ppermute | solution.py:394
  31.6 1.0 %collective-permute-start.10 = (bf16[144,384]{1,0:T(8,128)(2,1)S(1)}, bf16[144,384]{1,0:T(8,128)(2,1)S(1)}, u32[]{:S(2)}, u32[]{:S(2)}) collective-permute-start(bf16[144,384]{1,0:T(8,128)(2,1)S(1)} %collective-permute-done.6.refs_5_), channel_id=1, source_target_pairs={{0,2},{1,3},{2,0},{3,1},{4,6},{5,7},{6,4},{7,5},{8,10},{9,11},{10,... | collective-permute-start | bytes 331784 | tf_op jit(solution)/shard_map/ppermute | solution.py:394
  33.6 1.4 %shard_map.117 = (bf16[256,384]{1,0:T(8,128)(2,1)S(1)}, f32[256,128]{1,0:T(8,128)S(1)}, f32[256,128]{1,0:T(8,128)S(1)}, f32[256,384]{1,0:T(8,128)S(1)}) custom-call(bf16[384,384]{1,0:T(8,128)(2,1)S(1)} %get-tuple-element.30.score_ref, bf16[272,384]{1,0:T(8,128)(2,1)S(1)} %get-tuple-element.53.refs_0_, bf16[144,384]{1,0:T(8,128)(2,1)S(1)} %collective-permute-done.3.refs_1_, ...), custom_call_target="tpu_custom_call" | custom-call | flops 503316480 | bytes 983040 | tf_op jit(solution)/shard_map/pallas_call | solution.py:553
  35.5 1.0 %collective-permute-done.12.refs_10_ = bf16[272,384]{1,0:T(8,128)(2,1)S(1)} collective-permute-done((bf16[272,384]{1,0:T(8,128)(2,1)S(1)}, bf16[272,384]{1,0:T(8,128)(2,1)S(1)}, u32[]{:S(2)}, u32[]{:S(2)}) %collective-permute-start.12) | collective-permute-done | bytes 208928 | tf_op jit(solution)/shard_map/ppermute | solution.py:394
  36.7 4.3 %collective-permute-done.13.refs_11_ = bf16[272,384]{1,0:T(8,128)(2,1)S(1)} collective-permute-done((bf16[272,384]{1,0:T(8,128)(2,1)S(1)}, bf16[272,384]{1,0:T(8,128)(2,1)S(1)}, u32[]{:S(2)}, u32[]{:S(2)}) %collective-permute-start.13) | collective-permute-done | bytes 208928 | tf_op jit(solution)/shard_map/ppermute | solution.py:394
  40.9 2.6 %shard_map.118 = (bf16[256,384]{1,0:T(8,128)(2,1)S(1)}, bf16[256,384]{1,0:T(8,128)(2,1)S(1)}) custom-call(bf16[256,384]{1,0:T(8,128)(2,1)S(1)} %get-tuple-element.47.own_query_ref, f32[256,128]{1,0:T(8,128)S(1)} %get-tuple-element.48.peak_ref, f32[256,128]{1,0:T(8,128)S(1)} %get-tuple-element.49.sums_ref, f32[256,384]{1,0:T(8,128)S(1)} %get-tuple-element.50.added_ref, ...), custom_call_target="tpu_custom_call" | custom-call | flops 603979776 | bytes 1572864 | tf_op jit(solution)/shard_map/pallas_call | solution.py:572
  43.5 7.1 %collective-permute-start.14 = (bf16[256,384]{1,0:T(8,128)(2,1)S(1)}, bf16[256,384]{1,0:T(8,128)(2,1)S(1)}, u32[]{:S(2)}, u32[]{:S(2)}) collective-permute-start(bf16[256,384]{1,0:T(8,128)(2,1)S(1)} %get-tuple-element.56), channel_id=1, source_target_pairs={{0,1},{1,0},{2,3},{3,2},{4,5},{5,4},{6,7},{7,6},{8,9},{9,8},{10,11... | collective-permute-start | bytes 589832 | tf_op jit(solution)/shard_map/ppermute | solution.py:601
  50.7 1.1 %collective-permute-done.14.swap_ref = bf16[256,384]{1,0:T(8,128)(2,1)S(1)} collective-permute-done((bf16[256,384]{1,0:T(8,128)(2,1)S(1)}, bf16[256,384]{1,0:T(8,128)(2,1)S(1)}, u32[]{:S(2)}, u32[]{:S(2)}) %collective-permute-start.14) | collective-permute-done | bytes 196640 | tf_op jit(solution)/shard_map/ppermute | solution.py:601
  51.7 3.0 %shard_map.119 = bf16[2,4,192,128]{3,2,1,0:T(8,128)(2,1)} custom-call(bf16[256,384]{1,0:T(8,128)(2,1)S(1)} %get-tuple-element.55.mid_ref, bf16[256,384]{1,0:T(8,128)(2,1)S(1)} %collective-permute-done.14.swap_ref, bf16[3,3,192,384]{3,2,1,0:T(8,128)(2,1)S(1)} %bitcast.7), custom_call_target="tpu_custom_call" | custom-call | flops 1358954496 | bytes 1327104 | tf_op jit(solution)/shard_map/pallas_call | solution.py:604
  (27 shorter events, 2.5 us)
Async XLA Ops:
  0.6 11.9 %copy-start.4 = (f32[384]{0:T(512)S(1)}, f32[384]{0:T(512)}, u32[]{:S(2)}) copy-start(f32[384]{0:T(512)} %norm_gain_ref.1) | copy-start | bytes 4612
  0.6 11.9 %copy-start.5 = (f32[384]{0:T(512)S(1)}, f32[384]{0:T(512)}, u32[]{:S(2)}) copy-start(f32[384]{0:T(512)} %gain_ref.3) | copy-start | bytes 4612
  1.8 9.2 %collective-permute-start = (bf16[4,64,384]{2,1,0:T(8,128)(2,1)S(1)}, bf16[4,64,384]{2,1,0:T(8,128)(2,1)S(1)}, u32[]{:S(2)}, u32[]{:S(2)}) collective-permute-start(bf16[4,64,384]{2,1,0:T(8,128)(2,1)S(1)} %get-tuple-element.31), channel_id=1, source_target_pairs={{1,2},{3,4},{5,6},{7,8},{9,10},{11,12},{13,14},{2,1},{4,3},{6,5},{... | collective-permute-start | bytes 589832 | tf_op jit(solution)/shard_map/ppermute | solution.py:479
  6.3 4.7 %collective-permute-start.1 = (bf16[3,2,64,384]{3,2,1,0:T(8,128)(2,1)S(1)}, bf16[3,2,64,384]{3,2,1,0:T(8,128)(2,1)S(1)}, u32[]{:S(2)}, u32[]{:S(2)}) collective-permute-start(bf16[3,2,64,384]{3,2,1,0:T(8,128)(2,1)S(1)} %get-tuple-element.34), channel_id=1, source_target_pairs={{0,1},{1,0},{2,3},{3,2},{4,5},{5,4},{6,7},{7,6},{8,9},{9,8},{10,11... | collective-permute-start | bytes 884744 | tf_op jit(solution)/shard_map/ppermute | solution.py:480
  6.4 26.6 %copy-start = (bf16[384,384]{1,0:T(8,128)(2,1)S(1)}, bf16[384,384]{1,0:T(8,128)(2,1)}, u32[]{:S(2)}) copy-start(bf16[384,384]{1,0:T(8,128)(2,1)} %query_ref.1) | copy-start | bytes 884740
  6.4 26.6 %copy-start.1 = (bf16[384,384]{1,0:T(8,128)(2,1)S(1)}, bf16[384,384]{1,0:T(8,128)(2,1)}, u32[]{:S(2)}) copy-start(bf16[384,384]{1,0:T(8,128)(2,1)} %key_ref.1) | copy-start | bytes 884740
  6.5 26.6 %copy-start.2 = (bf16[384,384]{1,0:T(8,128)(2,1)S(1)}, bf16[384,384]{1,0:T(8,128)(2,1)}, u32[]{:S(2)}) copy-start(bf16[384,384]{1,0:T(8,128)(2,1)} %value_ref.1) | copy-start | bytes 884740
  6.5 26.6 %copy-start.3 = (bf16[384,384]{1,0:T(8,128)(2,1)S(1)}, bf16[384,384]{1,0:T(8,128)(2,1)}, u32[]{:S(2)}) copy-start(bf16[384,384]{1,0:T(8,128)(2,1)} %out_ref.1) | copy-start | bytes 884740
  10.2 41.5 %copy-start.6 = (bf16[3,3,384,192]{2,3,1,0:T(8,128)(2,1)S(1)}, bf16[3,3,384,192]{2,3,1,0:T(8,128)(2,1)}, u32[]{:S(2)}) copy-start(bf16[3,3,384,192]{2,3,1,0:T(8,128)(2,1)} %param.19) | copy-start | bytes 3981316
  11.0 1.4 %collective-permute-start.2 = (bf16[4,64,384]{2,1,0:T(8,128)(2,1)S(1)}, bf16[4,64,384]{2,1,0:T(8,128)(2,1)S(1)}, u32[]{:S(2)}, u32[]{:S(2)}) collective-permute-start(bf16[4,64,384]{2,1,0:T(8,128)(2,1)S(1)} %collective-permute-done.edge_ref), channel_id=1, source_target_pairs={{0,1},{1,0},{2,3},{3,2},{4,5},{5,4},{6,7},{7,6},{8,9},{9,8},{10,11... | collective-permute-start | bytes 589832 | tf_op jit(solution)/shard_map/ppermute | solution.py:507
  15.6 7.5 %collective-permute-start.5 = (bf16[272,384]{1,0:T(8,128)(2,1)S(1)}, bf16[272,384]{1,0:T(8,128)(2,1)S(1)}, u32[]{:S(2)}, u32[]{:S(2)}) collective-permute-start(bf16[272,384]{1,0:T(8,128)(2,1)S(1)} %get-tuple-element.53.refs_0_), channel_id=1, source_target_pairs={{0,2},{1,3},{2,0},{3,1},{4,6},{5,7},{6,4},{7,5},{8,10},{9,11},{10,... | collective-permute-start | bytes 626696 | tf_op jit(solution)/shard_map/ppermute | solution.py:394
  17.9 4.9 %collective-permute-start.4 = (bf16[144,384]{1,0:T(8,128)(2,1)S(1)}, bf16[144,384]{1,0:T(8,128)(2,1)S(1)}, u32[]{:S(2)}, u32[]{:S(2)}) collective-permute-start(bf16[144,384]{1,0:T(8,128)(2,1)S(1)} %get-tuple-element.39), channel_id=1, source_target_pairs={{0,4},{1,5},{2,6},{3,7},{4,12},{5,13},{6,14},{7,15},{8,0},{9,1},{1... | collective-permute-start | bytes 331784 | tf_op jit(solution)/shard_map/ppermute | solution.py:394
  19.2 6.4 %collective-permute-start.3 = (bf16[144,384]{1,0:T(8,128)(2,1)S(1)}, bf16[144,384]{1,0:T(8,128)(2,1)S(1)}, u32[]{:S(2)}, u32[]{:S(2)}) collective-permute-start(bf16[144,384]{1,0:T(8,128)(2,1)S(1)} %get-tuple-element.38), channel_id=1, source_target_pairs={{0,4},{1,5},{2,6},{3,7},{4,12},{5,13},{6,14},{7,15},{8,0},{9,1},{1... | collective-permute-start | bytes 331784 | tf_op jit(solution)/shard_map/ppermute | solution.py:394
  23.1 5.1 %collective-permute-start.8 = (bf16[144,384]{1,0:T(8,128)(2,1)S(1)}, bf16[144,384]{1,0:T(8,128)(2,1)S(1)}, u32[]{:S(2)}, u32[]{:S(2)}) collective-permute-start(bf16[144,384]{1,0:T(8,128)(2,1)S(1)} %collective-permute-done.4.refs_2_), channel_id=1, source_target_pairs={{0,4},{1,5},{2,6},{3,7},{4,12},{5,13},{6,14},{7,15},{8,0},{9,1},{1... | collective-permute-start | bytes 331784 | tf_op jit(solution)/shard_map/ppermute | solution.py:394
  24.4 3.8 %collective-permute-start.9 = (bf16[144,384]{1,0:T(8,128)(2,1)S(1)}, bf16[144,384]{1,0:T(8,128)(2,1)S(1)}, u32[]{:S(2)}, u32[]{:S(2)}) collective-permute-start(bf16[144,384]{1,0:T(8,128)(2,1)S(1)} %collective-permute-done.4.refs_2_), channel_id=1, source_target_pairs={{0,2},{1,3},{2,0},{3,1},{4,6},{5,7},{6,4},{7,5},{8,10},{9,11},{10,... | collective-permute-start | bytes 331784 | tf_op jit(solution)/shard_map/ppermute | solution.py:394
  25.6 5.7 %collective-permute-start.6 = (bf16[144,384]{1,0:T(8,128)(2,1)S(1)}, bf16[144,384]{1,0:T(8,128)(2,1)S(1)}, u32[]{:S(2)}, u32[]{:S(2)}) collective-permute-start(bf16[144,384]{1,0:T(8,128)(2,1)S(1)} %collective-permute-done.3.refs_1_), channel_id=1, source_target_pairs={{0,4},{1,5},{2,6},{3,7},{4,12},{5,13},{6,14},{7,15},{8,0},{9,1},{1... | collective-permute-start | bytes 331784 | tf_op jit(solution)/shard_map/ppermute | solution.py:394
  26.9 4.7 %collective-permute-start.7 = (bf16[144,384]{1,0:T(8,128)(2,1)S(1)}, bf16[144,384]{1,0:T(8,128)(2,1)S(1)}, u32[]{:S(2)}, u32[]{:S(2)}) collective-permute-start(bf16[144,384]{1,0:T(8,128)(2,1)S(1)} %collective-permute-done.3.refs_1_), channel_id=1, source_target_pairs={{0,2},{1,3},{2,0},{3,1},{4,6},{5,7},{6,4},{7,5},{8,10},{9,11},{10,... | collective-permute-start | bytes 331784 | tf_op jit(solution)/shard_map/ppermute | solution.py:394
  28.1 8.4 %collective-permute-start.12 = (bf16[272,384]{1,0:T(8,128)(2,1)S(1)}, bf16[272,384]{1,0:T(8,128)(2,1)S(1)}, u32[]{:S(2)}, u32[]{:S(2)}) collective-permute-start(bf16[272,384]{1,0:T(8,128)(2,1)S(1)} %get-tuple-element.53.refs_0_), channel_id=1, source_target_pairs={{0,8},{1,9},{2,10},{3,11},{4,0},{5,1},{6,2},{7,3},{8,12},{9,13},{1... | collective-permute-start | bytes 626696 | tf_op jit(solution)/shard_map/ppermute | solution.py:394
  28.2 12.8 %collective-permute-start.13 = (bf16[272,384]{1,0:T(8,128)(2,1)S(1)}, bf16[272,384]{1,0:T(8,128)(2,1)S(1)}, u32[]{:S(2)}, u32[]{:S(2)}) collective-permute-start(bf16[272,384]{1,0:T(8,128)(2,1)S(1)} %collective-permute-done.5.refs_7_), channel_id=1, source_target_pairs={{0,8},{1,9},{2,10},{3,11},{4,0},{5,1},{6,2},{7,3},{8,12},{9,13},{1... | collective-permute-start | bytes 626696 | tf_op jit(solution)/shard_map/ppermute | solution.py:394
  31.6 3.9 %collective-permute-start.10 = (bf16[144,384]{1,0:T(8,128)(2,1)S(1)}, bf16[144,384]{1,0:T(8,128)(2,1)S(1)}, u32[]{:S(2)}, u32[]{:S(2)}) collective-permute-start(bf16[144,384]{1,0:T(8,128)(2,1)S(1)} %collective-permute-done.6.refs_5_), channel_id=1, source_target_pairs={{0,2},{1,3},{2,0},{3,1},{4,6},{5,7},{6,4},{7,5},{8,10},{9,11},{10,... | collective-permute-start | bytes 331784 | tf_op jit(solution)/shard_map/ppermute | solution.py:394
  32.6 4.1 %collective-permute-start.11 = (bf16[144,384]{1,0:T(8,128)(2,1)S(1)}, bf16[144,384]{1,0:T(8,128)(2,1)S(1)}, u32[]{:S(2)}, u32[]{:S(2)}) collective-permute-start(bf16[144,384]{1,0:T(8,128)(2,1)S(1)} %collective-permute-done.8.refs_6_), channel_id=1, source_target_pairs={{0,2},{1,3},{2,0},{3,1},{4,6},{5,7},{6,4},{7,5},{8,10},{9,11},{10,... | collective-permute-start | bytes 331784 | tf_op jit(solution)/shard_map/ppermute | solution.py:394
  43.5 8.2 %collective-permute-start.14 = (bf16[256,384]{1,0:T(8,128)(2,1)S(1)}, bf16[256,384]{1,0:T(8,128)(2,1)S(1)}, u32[]{:S(2)}, u32[]{:S(2)}) collective-permute-start(bf16[256,384]{1,0:T(8,128)(2,1)S(1)} %get-tuple-element.56), channel_id=1, source_target_pairs={{0,1},{1,0},{2,3},{3,2},{4,5},{5,4},{6,7},{7,6},{8,9},{9,8},{10,11... | collective-permute-start | bytes 589832 | tf_op jit(solution)/shard_map/ppermute | solution.py:601

commit v2 on v1

--- a/solution.py
+++ b/solution.py
@@ -403,10 +403,12 @@
 
     here = {k: k for k in range(chips)}
     early, late = [([block], here)], []
-    own_again = [block]
-    crossed = last = None
+    back = crossed = last = None
+    if length > 1:
+        back = send([block], backward)
     if depth == 2:
         crossed = send([block], across)
+    ties = {(2, 0): back}
     steps = length - 2
     parts, origin = list(halves), here
     for step in range(1, steps + 1):
@@ -415,24 +417,22 @@
             places = [(parts, h)]
             if last:
                 places.append((last, h))
-            if step == 1 and h == 1:
-                places.append((own_again, 0))
-                if depth == 2:
-                    places.append((crossed, 0))
+            if ties.get((step, h)):
+                places.append((ties[(step, h)], 0))
             tie(*places)
         early.append((parts, origin))
         if depth == 2:
             last = send(parts, across)
             (late if step == steps else early).append((last, moved(origin, across)))
-    if length > 1:
-        late.append((send(own_again, backward), moved(here, backward)))
     if depth == 2:
         (early if length > 1 else late).append((crossed, moved(here, across)))
-        if length > 1:
-            if steps > 0:
-                crossed = list(crossed)
-                tie((crossed, 0), (parts, 1))
-            late.append((send(crossed, backward), moved(moved(here, across), backward)))
+    if last:
+        tie((early[0][0], 0), (last, 0))
+    if back:
+        origin = moved(here, backward)
+        early.append((back, origin))
+        if depth == 2:
+            late.append((send(back, across), moved(origin, across)))
     return early, late
 
 

time: 55.2 us -> 56 us (1.014)
  the two profiles are of different devices: /device:TPU:1 before, /device:TPU:11 now
where the time goes in v2:
time: 56 us; the launch traced here: 55.9 us
  starting transfers between devices  20 us (36%)
  waiting for transfers between devices  19.9 us (36%)
  Pallas kernels  15.1 us (27%)
  between operations  0.75 us (1%)
    ppermute x11, waiting for transfers between devices, send(): return [lax.ppermute(part, 'rows', pairs) for part in parts]  15.9 us
    ppermute x11, starting transfers between devices, send(): return [lax.ppermute(part, 'rows', pairs) for part in parts]  13.2 us
    pallas_call x1, Pallas kernels, shards(): pl.pallas_call(prepare_kernel, out_shape=(jax.ShapeDtypeStruct((frames, o...  3.76 us
    ppermute x1, starting transfers between devices, shards(): edge_rows = lax.ppermute(edge_rows, 'rows', neighbour)  3.71 us
    ppermute x1, starting transfers between devices, shards(): swap_rows = lax.ppermute(swap_rows, 'rows', swap)  3.08 us
    pallas_call x1, Pallas kernels, shards(): pl.pallas_call(functools.partial(conv_kernel, width), out_shape=(block, h...  3.08 us
    pallas_call x1, Pallas kernels, shards(): pl.pallas_call(functools.partial(up_kernel, width), out_shape=jax.ShapeDt...  2.94 us
    pallas_call x1, Pallas kernels, shards(): pl.pallas_call(functools.partial(late_kernel, width, sources, counts, len...  2.28 us
  transfers between devices with their start and end apart: 15, of which 8 were waited for; matrix products, arithmetic and copies ran while one was open for 0% of the time, Pallas kernels for 10%

profile of v2, /device:TPU:11, one launch (start us, length us, event | category | flops | bytes accessed | tf_op | source)
XLA Modules:
  0.0 55.9 jit_solution(8132928860527039635)
XLA Ops:
  0.7 1.1 %shard_map.114 = (bf16[4,64,384]{2,1,0:T(8,128)(2,1)S(1)}, bf16[3,2,64,384]{3,2,1,0:T(8,128)(2,1)S(1)}) custom-call(bf16[2,2,64,384]{3,2,1,0:T(8,128)(2,1)} %latents_ref.1, bf16[2,2,64,384]{3,2,1,0:T(8,128)(2,1)} %cache_ref.1), custom_call_target="tpu_custom_call" | custom-call | bytes 491520 | tf_op jit(solution)/shard_map/pallas_call | solution.py:467
  1.8 3.7 %collective-permute-start = (bf16[4,64,384]{2,1,0:T(8,128)(2,1)S(1)}, bf16[4,64,384]{2,1,0:T(8,128)(2,1)S(1)}, u32[]{:S(2)}, u32[]{:S(2)}) collective-permute-start(bf16[4,64,384]{2,1,0:T(8,128)(2,1)S(1)} %get-tuple-element.29), channel_id=1, source_target_pairs={{1,2},{3,4},{5,6},{7,8},{9,10},{11,12},{13,14},{2,1},{4,3},{6,5},{... | collective-permute-start | bytes 589832 | tf_op jit(solution)/shard_map/ppermute | solution.py:479
  5.6 3.8 %shard_map.115 = (bf16[2,128,384]{2,1,0:T(8,128)(2,1)}, bf16[3,128,384]{2,1,0:T(8,128)(2,1)S(1)}, bf16[3,3,384,1152]{3,2,1,0:T(8,128)(2,1)S(1)}) custom-call(bf16[2,128,384]{2,1,0:T(8,128)(2,1)} %bitcast.8, bf16[2,128,384]{2,1,0:T(8,128)(2,1)} %bitcast.9, bf16[3,3,3,384,384]{4,3,2,1,0:T(8,128)(2,1)} %weight_ref.1, f32[384]{0:T(512)} %norm_gain_ref.1), custom_call_target="tpu_custom_call" | custom-call | flops 983040 | bytes 7962624 | tf_op jit(solution)/shard_map/pallas_call | solution.py:481
  9.4 1.6 %collective-permute-done.edge_ref = bf16[4,64,384]{2,1,0:T(8,128)(2,1)S(1)} collective-permute-done((bf16[4,64,384]{2,1,0:T(8,128)(2,1)S(1)}, bf16[4,64,384]{2,1,0:T(8,128)(2,1)S(1)}, u32[]{:S(2)}, u32[]{:S(2)}) %collective-permute-start) | collective-permute-done | bytes 196640 | tf_op jit(solution)/shard_map/ppermute | solution.py:479
  11.0 1.4 %collective-permute-done.2.far_ref = bf16[4,64,384]{2,1,0:T(8,128)(2,1)S(1)} collective-permute-done((bf16[4,64,384]{2,1,0:T(8,128)(2,1)S(1)}, bf16[4,64,384]{2,1,0:T(8,128)(2,1)S(1)}, u32[]{:S(2)}, u32[]{:S(2)}) %collective-permute-start.2) | collective-permute-done | bytes 196640 | tf_op jit(solution)/shard_map/ppermute | solution.py:507
  12.4 3.1 %shard_map.116 = (bf16[272,384]{1,0:T(8,128)(2,1)S(1)}, bf16[144,384]{1,0:T(8,128)(2,1)S(1)}, bf16[144,384]{1,0:T(8,128)(2,1)S(1)}, f32[256,384]{1,0:T(8,128)S(1)}) custom-call(bf16[3,128,384]{2,1,0:T(8,128)(2,1)S(1)} %get-tuple-element.31.own_ref, bf16[3,128,384]{2,1,0:T(8,128)(2,1)S(1)} %bitcast.6, bf16[4,64,384]{2,1,0:T(8,128)(2,1)S(1)} %collective-permute-done.edge_ref, ...), custom_call_target="tpu_custom_call" | custom-call | flops 2038431744 | bytes 7962624 | tf_op jit(solution)/shard_map/pallas_call | solution.py:510
  15.5 2.4 %collective-permute-start.3 = (bf16[144,384]{1,0:T(8,128)(2,1)S(1)}, bf16[144,384]{1,0:T(8,128)(2,1)S(1)}, u32[]{:S(2)}, u32[]{:S(2)}) collective-permute-start(bf16[144,384]{1,0:T(8,128)(2,1)S(1)} %get-tuple-element.36), channel_id=1, source_target_pairs={{0,4},{1,5},{2,6},{3,7},{4,12},{5,13},{6,14},{7,15},{8,0},{9,1},{1... | collective-permute-start | bytes 331784 | tf_op jit(solution)/shard_map/ppermute | solution.py:394
  17.9 2.4 %collective-permute-start.8 = (bf16[144,384]{1,0:T(8,128)(2,1)S(1)}, bf16[144,384]{1,0:T(8,128)(2,1)S(1)}, u32[]{:S(2)}, u32[]{:S(2)}) collective-permute-start(bf16[144,384]{1,0:T(8,128)(2,1)S(1)} %get-tuple-element.39), channel_id=1, source_target_pairs={{0,4},{1,5},{2,6},{3,7},{4,12},{5,13},{6,14},{7,15},{8,0},{9,1},{1... | collective-permute-start | bytes 331784 | tf_op jit(solution)/shard_map/ppermute | solution.py:394
  20.2 3.9 %collective-permute-done.3.refs_1_ = bf16[144,384]{1,0:T(8,128)(2,1)S(1)} collective-permute-done((bf16[144,384]{1,0:T(8,128)(2,1)S(1)}, bf16[144,384]{1,0:T(8,128)(2,1)S(1)}, u32[]{:S(2)}, u32[]{:S(2)}) %collective-permute-start.3) | collective-permute-done | bytes 110624 | tf_op jit(solution)/shard_map/ppermute | solution.py:394
  24.1 3.6 %collective-permute-start.4 = (bf16[144,384]{1,0:T(8,128)(2,1)S(1)}, bf16[144,384]{1,0:T(8,128)(2,1)S(1)}, u32[]{:S(2)}, u32[]{:S(2)}) collective-permute-start(bf16[144,384]{1,0:T(8,128)(2,1)S(1)} %collective-permute-done.3.refs_1_), channel_id=1, source_target_pairs={{0,4},{1,5},{2,6},{3,7},{4,12},{5,13},{6,14},{7,15},{8,0},{9,1},{1... | collective-permute-start | bytes 331784 | tf_op jit(solution)/shard_map/ppermute | solution.py:394
  27.7 1.5 %collective-permute-start.11 = (bf16[272,384]{1,0:T(8,128)(2,1)S(1)}, bf16[272,384]{1,0:T(8,128)(2,1)S(1)}, u32[]{:S(2)}, u32[]{:S(2)}) collective-permute-start(bf16[272,384]{1,0:T(8,128)(2,1)S(1)} %get-tuple-element.38.refs_0_), channel_id=1, source_target_pairs={{0,2},{1,3},{2,0},{3,1},{4,6},{5,7},{6,4},{7,5},{8,10},{9,11},{10,... | collective-permute-start | bytes 626696 | tf_op jit(solution)/shard_map/ppermute | solution.py:394
  29.2 0.9 %collective-permute-start.9 = (bf16[144,384]{1,0:T(8,128)(2,1)S(1)}, bf16[144,384]{1,0:T(8,128)(2,1)S(1)}, u32[]{:S(2)}, u32[]{:S(2)}) collective-permute-start(bf16[144,384]{1,0:T(8,128)(2,1)S(1)} %collective-permute-done.8.refs_2_), channel_id=1, source_target_pairs={{0,4},{1,5},{2,6},{3,7},{4,12},{5,13},{6,14},{7,15},{8,0},{9,1},{1... | collective-permute-start | bytes 331784 | tf_op jit(solution)/shard_map/ppermute | solution.py:394
  30.1 1.2 %collective-permute-done.5.refs_3_ = bf16[144,384]{1,0:T(8,128)(2,1)S(1)} collective-permute-done((bf16[144,384]{1,0:T(8,128)(2,1)S(1)}, bf16[144,384]{1,0:T(8,128)(2,1)S(1)}, u32[]{:S(2)}, u32[]{:S(2)}) %collective-permute-start.5) | collective-permute-done | bytes 110624 | tf_op jit(solution)/shard_map/ppermute | solution.py:394
  31.6 1.2 %collective-permute-start.7 = (bf16[144,384]{1,0:T(8,128)(2,1)S(1)}, bf16[144,384]{1,0:T(8,128)(2,1)S(1)}, u32[]{:S(2)}, u32[]{:S(2)}) collective-permute-start(bf16[144,384]{1,0:T(8,128)(2,1)S(1)} %collective-permute-done.4.refs_5_), channel_id=1, source_target_pairs={{0,2},{1,3},{2,0},{3,1},{4,6},{5,7},{6,4},{7,5},{8,10},{9,11},{10,... | collective-permute-start | bytes 331784 | tf_op jit(solution)/shard_map/ppermute | solution.py:394
  32.8 4.5 %collective-permute-done.10.refs_4_ = bf16[144,384]{1,0:T(8,128)(2,1)S(1)} collective-permute-done((bf16[144,384]{1,0:T(8,128)(2,1)S(1)}, bf16[144,384]{1,0:T(8,128)(2,1)S(1)}, u32[]{:S(2)}, u32[]{:S(2)}) %collective-permute-start.10) | collective-permute-done | bytes 110624 | tf_op jit(solution)/shard_map/ppermute | solution.py:394
  37.3 1.0 %collective-permute-start.12 = (bf16[144,384]{1,0:T(8,128)(2,1)S(1)}, bf16[144,384]{1,0:T(8,128)(2,1)S(1)}, u32[]{:S(2)}, u32[]{:S(2)}) collective-permute-start(bf16[144,384]{1,0:T(8,128)(2,1)S(1)} %collective-permute-done.9.refs_6_), channel_id=1, source_target_pairs={{0,2},{1,3},{2,0},{3,1},{4,6},{5,7},{6,4},{7,5},{8,10},{9,11},{10,... | collective-permute-start | bytes 331784 | tf_op jit(solution)/shard_map/ppermute | solution.py:394
  38.3 0.5 shard_map.113
  38.8 5.3 %collective-permute-done.7.refs_9_ = bf16[144,384]{1,0:T(8,128)(2,1)S(1)} collective-permute-done((bf16[144,384]{1,0:T(8,128)(2,1)S(1)}, bf16[144,384]{1,0:T(8,128)(2,1)S(1)}, u32[]{:S(2)}, u32[]{:S(2)}) %collective-permute-start.7) | collective-permute-done | bytes 110624 | tf_op jit(solution)/shard_map/ppermute | solution.py:394
  44.1 1.4 %shard_map.117 = (bf16[256,384]{1,0:T(8,128)(2,1)S(1)}, f32[256,128]{1,0:T(8,128)S(1)}, f32[256,128]{1,0:T(8,128)S(1)}, f32[256,384]{1,0:T(8,128)S(1)}) custom-call(bf16[384,384]{1,0:T(8,128)(2,1)S(1)} %get-tuple-element.28.score_ref, bf16[272,384]{1,0:T(8,128)(2,1)S(1)} %get-tuple-element.38.refs_0_, bf16[144,384]{1,0:T(8,128)(2,1)S(1)} %collective-permute-done.3.refs_1_, ...), custom_call_target="tpu_custom_call" | custom-call | flops 603979776 | bytes 1179648 | tf_op jit(solution)/shard_map/pallas_call | solution.py:553
  45.5 1.0 %collective-permute-done.12.refs_10_ = bf16[144,384]{1,0:T(8,128)(2,1)S(1)} collective-permute-done((bf16[144,384]{1,0:T(8,128)(2,1)S(1)}, bf16[144,384]{1,0:T(8,128)(2,1)S(1)}, u32[]{:S(2)}, u32[]{:S(2)}) %collective-permute-start.12) | collective-permute-done | bytes 110624 | tf_op jit(solution)/shard_map/ppermute | solution.py:394
  46.5 2.3 %shard_map.118 = (bf16[256,384]{1,0:T(8,128)(2,1)S(1)}, bf16[256,384]{1,0:T(8,128)(2,1)S(1)}) custom-call(bf16[256,384]{1,0:T(8,128)(2,1)S(1)} %get-tuple-element.44.own_query_ref, f32[256,128]{1,0:T(8,128)S(1)} %get-tuple-element.45.peak_ref, f32[256,128]{1,0:T(8,128)S(1)} %get-tuple-element.46.sums_ref, f32[256,384]{1,0:T(8,128)S(1)} %get-tuple-element.47.added_ref, ...), custom_call_target="tpu_custom_call" | custom-call | flops 603979776 | bytes 1572864 | tf_op jit(solution)/shard_map/pallas_call | solution.py:572
  48.8 3.1 %collective-permute-start.14 = (bf16[256,384]{1,0:T(8,128)(2,1)S(1)}, bf16[256,384]{1,0:T(8,128)(2,1)S(1)}, u32[]{:S(2)}, u32[]{:S(2)}) collective-permute-start(bf16[256,384]{1,0:T(8,128)(2,1)S(1)} %get-tuple-element.52), channel_id=1, source_target_pairs={{0,1},{1,0},{2,3},{3,2},{4,5},{5,4},{6,7},{7,6},{8,9},{9,8},{10,11... | collective-permute-start | bytes 589832 | tf_op jit(solution)/shard_map/ppermute | solution.py:601
  51.9 1.1 %collective-permute-done.14.swap_ref = bf16[256,384]{1,0:T(8,128)(2,1)S(1)} collective-permute-done((bf16[256,384]{1,0:T(8,128)(2,1)S(1)}, bf16[256,384]{1,0:T(8,128)(2,1)S(1)}, u32[]{:S(2)}, u32[]{:S(2)}) %collective-permute-start.14) | collective-permute-done | bytes 196640 | tf_op jit(solution)/shard_map/ppermute | solution.py:601
  52.9 2.9 %shard_map.119 = bf16[2,4,192,128]{3,2,1,0:T(8,128)(2,1)} custom-call(bf16[256,384]{1,0:T(8,128)(2,1)S(1)} %get-tuple-element.51.mid_ref, bf16[256,384]{1,0:T(8,128)(2,1)S(1)} %collective-permute-done.14.swap_ref, bf16[3,3,192,384]{3,2,1,0:T(8,128)(2,1)S(1)} %bitcast.7), custom_call_target="tpu_custom_call" | custom-call | flops 1358954496 | bytes 1327104 | tf_op jit(solution)/shard_map/pallas_call | solution.py:604
  (27 shorter events, 0.5 us)
Async XLA Ops:
  0.6 11.8 %copy-start.4 = (f32[384]{0:T(512)S(1)}, f32[384]{0:T(512)}, u32[]{:S(2)}) copy-start(f32[384]{0:T(512)} %norm_gain_ref.1) | copy-start | bytes 4612
  0.6 11.8 %copy-start.5 = (f32[384]{0:T(512)S(1)}, f32[384]{0:T(512)}, u32[]{:S(2)}) copy-start(f32[384]{0:T(512)} %gain_ref.3) | copy-start | bytes 4612
  1.8 9.2 %collective-permute-start = (bf16[4,64,384]{2,1,0:T(8,128)(2,1)S(1)}, bf16[4,64,384]{2,1,0:T(8,128)(2,1)S(1)}, u32[]{:S(2)}, u32[]{:S(2)}) collective-permute-start(bf16[4,64,384]{2,1,0:T(8,128)(2,1)S(1)} %get-tuple-element.29), channel_id=1, source_target_pairs={{1,2},{3,4},{5,6},{7,8},{9,10},{11,12},{13,14},{2,1},{4,3},{6,5},{... | collective-permute-start | bytes 589832 | tf_op jit(solution)/shard_map/ppermute | solution.py:479
  5.5 5.5 %collective-permute-start.1 = (bf16[3,2,64,384]{3,2,1,0:T(8,128)(2,1)S(1)}, bf16[3,2,64,384]{3,2,1,0:T(8,128)(2,1)S(1)}, u32[]{:S(2)}, u32[]{:S(2)}) collective-permute-start(bf16[3,2,64,384]{3,2,1,0:T(8,128)(2,1)S(1)} %get-tuple-element.32), channel_id=1, source_target_pairs={{0,1},{1,0},{2,3},{3,2},{4,5},{5,4},{6,7},{7,6},{8,9},{9,8},{10,11... | collective-permute-start | bytes 884744 | tf_op jit(solution)/shard_map/ppermute | solution.py:480
  5.6 32.7 %copy-start = (bf16[384,384]{1,0:T(8,128)(2,1)S(1)}, bf16[384,384]{1,0:T(8,128)(2,1)}, u32[]{:S(2)}) copy-start(bf16[384,384]{1,0:T(8,128)(2,1)} %query_ref.1) | copy-start | bytes 884740
  5.6 32.6 %copy-start.1 = (bf16[384,384]{1,0:T(8,128)(2,1)S(1)}, bf16[384,384]{1,0:T(8,128)(2,1)}, u32[]{:S(2)}) copy-start(bf16[384,384]{1,0:T(8,128)(2,1)} %key_ref.1) | copy-start | bytes 884740
  5.6 32.6 %copy-start.2 = (bf16[384,384]{1,0:T(8,128)(2,1)S(1)}, bf16[384,384]{1,0:T(8,128)(2,1)}, u32[]{:S(2)}) copy-start(bf16[384,384]{1,0:T(8,128)(2,1)} %value_ref.1) | copy-start | bytes 884740
  5.6 32.6 %copy-start.3 = (bf16[384,384]{1,0:T(8,128)(2,1)S(1)}, bf16[384,384]{1,0:T(8,128)(2,1)}, u32[]{:S(2)}) copy-start(bf16[384,384]{1,0:T(8,128)(2,1)} %out_ref.1) | copy-start | bytes 884740
  11.0 1.4 %collective-permute-start.2 = (bf16[4,64,384]{2,1,0:T(8,128)(2,1)S(1)}, bf16[4,64,384]{2,1,0:T(8,128)(2,1)S(1)}, u32[]{:S(2)}, u32[]{:S(2)}) collective-permute-start(bf16[4,64,384]{2,1,0:T(8,128)(2,1)S(1)} %collective-permute-done.edge_ref), channel_id=1, source_target_pairs={{0,1},{1,0},{2,3},{3,2},{4,5},{5,4},{6,7},{7,6},{8,9},{9,8},{10,11... | collective-permute-start | bytes 589832 | tf_op jit(solution)/shard_map/ppermute | solution.py:507
  12.4 40.5 %copy-start.6 = (bf16[3,3,384,192]{2,3,1,0:T(8,128)(2,1)S(1)}, bf16[3,3,384,192]{2,3,1,0:T(8,128)(2,1)}, u32[]{:S(2)}) copy-start(bf16[3,3,384,192]{2,3,1,0:T(8,128)(2,1)} %param.19) | copy-start | bytes 3981316
  15.5 8.6 %collective-permute-start.3 = (bf16[144,384]{1,0:T(8,128)(2,1)S(1)}, bf16[144,384]{1,0:T(8,128)(2,1)S(1)}, u32[]{:S(2)}, u32[]{:S(2)}) collective-permute-start(bf16[144,384]{1,0:T(8,128)(2,1)S(1)} %get-tuple-element.36), channel_id=1, source_target_pairs={{0,4},{1,5},{2,6},{3,7},{4,12},{5,13},{6,14},{7,15},{8,0},{9,1},{1... | collective-permute-start | bytes 331784 | tf_op jit(solution)/shard_map/ppermute | solution.py:394
  17.9 11.4 %collective-permute-start.6 = (bf16[272,384]{1,0:T(8,128)(2,1)S(1)}, bf16[272,384]{1,0:T(8,128)(2,1)S(1)}, u32[]{:S(2)}, u32[]{:S(2)}) collective-permute-start(bf16[272,384]{1,0:T(8,128)(2,1)S(1)} %get-tuple-element.38.refs_0_), channel_id=1, source_target_pairs={{0,8},{1,9},{2,10},{3,11},{4,0},{5,1},{6,2},{7,3},{8,12},{9,13},{1... | collective-permute-start | bytes 626696 | tf_op jit(solution)/shard_map/ppermute | solution.py:394
  17.9 11.3 %collective-permute-start.8 = (bf16[144,384]{1,0:T(8,128)(2,1)S(1)}, bf16[144,384]{1,0:T(8,128)(2,1)S(1)}, u32[]{:S(2)}, u32[]{:S(2)}) collective-permute-start(bf16[144,384]{1,0:T(8,128)(2,1)S(1)} %get-tuple-element.39), channel_id=1, source_target_pairs={{0,4},{1,5},{2,6},{3,7},{4,12},{5,13},{6,14},{7,15},{8,0},{9,1},{1... | collective-permute-start | bytes 331784 | tf_op jit(solution)/shard_map/ppermute | solution.py:394
  24.1 6.0 %collective-permute-start.4 = (bf16[144,384]{1,0:T(8,128)(2,1)S(1)}, bf16[144,384]{1,0:T(8,128)(2,1)S(1)}, u32[]{:S(2)}, u32[]{:S(2)}) collective-permute-start(bf16[144,384]{1,0:T(8,128)(2,1)S(1)} %collective-permute-done.3.refs_1_), channel_id=1, source_target_pairs={{0,4},{1,5},{2,6},{3,7},{4,12},{5,13},{6,14},{7,15},{8,0},{9,1},{1... | collective-permute-start | bytes 331784 | tf_op jit(solution)/shard_map/ppermute | solution.py:394
  27.7 3.6 %collective-permute-start.5 = (bf16[144,384]{1,0:T(8,128)(2,1)S(1)}, bf16[144,384]{1,0:T(8,128)(2,1)S(1)}, u32[]{:S(2)}, u32[]{:S(2)}) collective-permute-start(bf16[144,384]{1,0:T(8,128)(2,1)S(1)} %collective-permute-done.3.refs_1_), channel_id=1, source_target_pairs={{0,2},{1,3},{2,0},{3,1},{4,6},{5,7},{6,4},{7,5},{8,10},{9,11},{10,... | collective-permute-start | bytes 331784 | tf_op jit(solution)/shard_map/ppermute | solution.py:394
  27.7 16.4 %collective-permute-start.11 = (bf16[272,384]{1,0:T(8,128)(2,1)S(1)}, bf16[272,384]{1,0:T(8,128)(2,1)S(1)}, u32[]{:S(2)}, u32[]{:S(2)}) collective-permute-start(bf16[272,384]{1,0:T(8,128)(2,1)S(1)} %get-tuple-element.38.refs_0_), channel_id=1, source_target_pairs={{0,2},{1,3},{2,0},{3,1},{4,6},{5,7},{6,4},{7,5},{8,10},{9,11},{10,... | collective-permute-start | bytes 626696 | tf_op jit(solution)/shard_map/ppermute | solution.py:394
  29.2 8.1 %collective-permute-start.10 = (bf16[144,384]{1,0:T(8,128)(2,1)S(1)}, bf16[144,384]{1,0:T(8,128)(2,1)S(1)}, u32[]{:S(2)}, u32[]{:S(2)}) collective-permute-start(bf16[144,384]{1,0:T(8,128)(2,1)S(1)} %collective-permute-done.8.refs_2_), channel_id=1, source_target_pairs={{0,2},{1,3},{2,0},{3,1},{4,6},{5,7},{6,4},{7,5},{8,10},{9,11},{10,... | collective-permute-start | bytes 331784 | tf_op jit(solution)/shard_map/ppermute | solution.py:394
  29.2 8.0 %collective-permute-start.9 = (bf16[144,384]{1,0:T(8,128)(2,1)S(1)}, bf16[144,384]{1,0:T(8,128)(2,1)S(1)}, u32[]{:S(2)}, u32[]{:S(2)}) collective-permute-start(bf16[144,384]{1,0:T(8,128)(2,1)S(1)} %collective-permute-done.8.refs_2_), channel_id=1, source_target_pairs={{0,4},{1,5},{2,6},{3,7},{4,12},{5,13},{6,14},{7,15},{8,0},{9,1},{1... | collective-permute-start | bytes 331784 | tf_op jit(solution)/shard_map/ppermute | solution.py:394
  31.3 15.2 %collective-permute-start.13 = (bf16[272,384]{1,0:T(8,128)(2,1)S(1)}, bf16[272,384]{1,0:T(8,128)(2,1)S(1)}, u32[]{:S(2)}, u32[]{:S(2)}) collective-permute-start(bf16[272,384]{1,0:T(8,128)(2,1)S(1)} %collective-permute-done.6.refs_8_), channel_id=1, source_target_pairs={{0,2},{1,3},{2,0},{3,1},{4,6},{5,7},{6,4},{7,5},{8,10},{9,11},{10,... | collective-permute-start | bytes 626696 | tf_op jit(solution)/shard_map/ppermute | solution.py:394
  31.6 12.5 %collective-permute-start.7 = (bf16[144,384]{1,0:T(8,128)(2,1)S(1)}, bf16[144,384]{1,0:T(8,128)(2,1)S(1)}, u32[]{:S(2)}, u32[]{:S(2)}) collective-permute-start(bf16[144,384]{1,0:T(8,128)(2,1)S(1)} %collective-permute-done.4.refs_5_), channel_id=1, source_target_pairs={{0,2},{1,3},{2,0},{3,1},{4,6},{5,7},{6,4},{7,5},{8,10},{9,11},{10,... | collective-permute-start | bytes 331784 | tf_op jit(solution)/shard_map/ppermute | solution.py:394
  37.3 9.2 %collective-permute-start.12 = (bf16[144,384]{1,0:T(8,128)(2,1)S(1)}, bf16[144,384]{1,0:T(8,128)(2,1)S(1)}, u32[]{:S(2)}, u32[]{:S(2)}) collective-permute-start(bf16[144,384]{1,0:T(8,128)(2,1)S(1)} %collective-permute-done.9.refs_6_), channel_id=1, source_target_pairs={{0,2},{1,3},{2,0},{3,1},{4,6},{5,7},{6,4},{7,5},{8,10},{9,11},{10,... | collective-permute-start | bytes 331784 | tf_op jit(solution)/shard_map/ppermute | solution.py:394
  48.8 4.2 %collective-permute-start.14 = (bf16[256,384]{1,0:T(8,128)(2,1)S(1)}, bf16[256,384]{1,0:T(8,128)(2,1)S(1)}, u32[]{:S(2)}, u32[]{:S(2)}) collective-permute-start(bf16[256,384]{1,0:T(8,128)(2,1)S(1)} %get-tuple-element.52), channel_id=1, source_target_pairs={{0,1},{1,0},{2,3},{3,2},{4,5},{5,4},{6,7},{7,6},{8,9},{9,8},{10,11... | collective-permute-start | bytes 589832 | tf_op jit(solution)/shard_map/ppermute | solution.py:601
